TPU v7x, 32 devices: a whole 2x2x4 slice. The times are simulated.
32 devices in a mesh: dp: 4 (over x, core), expert: 8 (over z, y).
Axes of the slice: x: 2, y: 2, z: 4, core: 2. Of those that a mesh axis runs over, the one named last changes fastest.
Arguments:
- grad_out: bfloat16 [4096, 3584], P(('dp', 'expert')), may hold values from -1.5 to 1.5
- gate_probs: float32 [4096, 4], P(('dp', 'expert')), may hold values from 0.05 to 0.3
- expert_route: int32 [4096, 4], P(('dp', 'expert')), may hold values from 0 to 11, all different within a row; in each aligned block of 128 rows (0 to 127, 128 to 255, ...) at most 48 rows name the same one
- replica_pick: int32 [4096, 4], P(('dp', 'expert')), may hold values from 0 to 59
- slot_expert: int32 [16], replicated, may hold values from 0 to 11, as said below
- saved_hidden: bfloat16 [4, 8, 8, 2, 48, 1024], P('dp', 'expert'), may hold values from -6 to 6
- master: float32 [16, 1024, 3584], P('expert', 'dp'), as said below
- first_moment: bfloat16 [16, 1024, 3584], P('expert', 'dp'), as said below
- second_moment: bfloat16 [16, 1024, 3584], P('expert', 'dp'), as said below
Outputs:
- hidden_grad: bfloat16 [4, 8, 8, 2, 48, 1024], P('dp', 'expert')
- gate_grad: float32 [4096, 4], P(('dp', 'expert'))
- new_master: float32 [16, 1024, 3584], P('expert', 'dp')
- new_first: bfloat16 [16, 1024, 3584], P('expert', 'dp')
- new_second: bfloat16 [16, 1024, 3584], P('expert', 'dp')
Inputs may be any that keep to these rules, and one draw needn't show every extreme that they name: `expert_route`: each row names 4 different experts; in the rows of one device no expert is named more than 48 times, a bound that some block reaches. `slot_expert`: every expert has at least one slot; experts 0 to 2 have two or more slots each, every other expert exactly one. `master`: slots holding the same expert hold equal values. `first_moment`: slots holding the same expert hold equal values. `second_moment`: slots holding the same expert hold equal values; all entries are positive.
All inputs are finite; a program needn't handle non-finite values.
Results may differ from a plain program's by a relative error of at most 0.017.
Values may be sent and summed in bfloat16 or wider, within the bound.
No kernel may reach another device: no remote copies, remote signals or barrier semaphores. Data moves between devices by JAX's collectives and lax.ppermute only.
A program may use at most 128 MiB of HBM per device.

v0:
```python
import jax
import jax.numpy as jnp
from jax import lax
from jax.sharding import PartitionSpec as P

HOT = 3


beta_one = 0.9
beta_two = 0.95
learn_rate = 0.00022
decay_rate = 0.1
epsilon = 1e-08
correct_one = 0.6513215599
correct_two = 0.4012630607


def on_device(
    grad_out,
    gate_probs,
    expert_route,
    replica_pick,
    slot_expert,
    saved_hidden,
    master,
    first_moment,
    second_moment,
):
    dev_count = lax.axis_size("expert")
    slot_count = slot_expert.shape[0]
    slot_dev = slot_count // dev_count
    capacity = saved_hidden.shape[4]
    feature_count = grad_out.shape[1]
    tok_rows, top_count = gate_probs.shape
    assigned = tok_rows * top_count
    shard_rows = master.shape[1]
    slot_ids = jnp.arange(slot_count, dtype=jnp.int32)
    same_expert = slot_expert[:, None] == slot_expert[None, :]
    slot_rank = jnp.sum(same_expert & (slot_ids[None, :] < slot_ids[:, None]), axis=1)
    experts_flat = expert_route.reshape(assigned)
    replica_picks = replica_pick.reshape(assigned)
    host_mask = slot_expert[None, :] == experts_flat[:, None]
    copy_count = jnp.sum(host_mask.astype(jnp.int32), axis=1)
    chosen = host_mask & (slot_rank[None, :] == (replica_picks % copy_count)[:, None])
    target = jnp.sum(jnp.where(chosen, slot_ids[None, :], 0), axis=1)
    onehot = (target[:, None] == slot_ids[None, :]).astype(jnp.int32)
    position = jnp.sum(onehot * (jnp.cumsum(onehot, axis=0) - onehot), axis=1)
    dest_index = target * capacity + position
    repeated = jnp.repeat(grad_out, top_count, axis=0)
    send_rows = (
        jnp.zeros((slot_count * capacity, feature_count), jnp.bfloat16).at[dest_index].set(repeated)
    )
    send_gates = (
        jnp.zeros((slot_count * capacity,), jnp.bfloat16)
        .at[dest_index]
        .set(gate_probs.reshape(assigned).astype(jnp.bfloat16))
    )
    recv_rows, recv_gates = (
        lax.all_to_all(
            send_rows.reshape(dev_count, slot_dev, capacity, feature_count),
            "expert",
            split_axis=0,
            concat_axis=0,
            tiled=True,
        ),
        lax.all_to_all(
            send_gates.reshape(dev_count, slot_dev, capacity),
            "expert",
            split_axis=0,
            concat_axis=0,
            tiled=True,
        ),
    )
    hidden = saved_hidden[0, 0]
    weights = master.astype(jnp.bfloat16)
    projected = jnp.einsum(
        "qlcd,lhd->qlch",
        recv_rows,
        lax.all_gather(weights, "dp", axis=1, tiled=True),
        preferred_element_type=jnp.float32,
    )
    gate_scale = recv_gates.astype(jnp.float32)[..., None]
    hidden_grad = (gate_scale * projected).astype(jnp.bfloat16)
    gate_terms = jnp.sum(hidden.astype(jnp.float32) * projected, axis=-1)
    returned = lax.all_to_all(gate_terms, "expert", split_axis=0, concat_axis=0, tiled=True)
    gate_grad = returned.reshape(slot_count * capacity)[dest_index].reshape(tok_rows, top_count)
    scaled = (gate_scale * recv_rows.astype(jnp.float32)).astype(jnp.bfloat16)
    reduced = lax.psum_scatter(
        jnp.einsum("qlch,qlcd->hld", hidden, scaled, preferred_element_type=jnp.float32).astype(
            jnp.bfloat16
        ),
        "dp",
        scatter_dimension=0,
        tiled=True,
    ).astype(jnp.float32)
    local_grad = jnp.transpose(reduced, (1, 0, 2))
    flat_grad = local_grad.reshape(slot_dev, shard_rows * feature_count)
    own_slots = lax.dynamic_slice_in_dim(slot_expert, lax.axis_index("expert") * slot_dev, slot_dev)
    hot_ids = jnp.arange(HOT, dtype=jnp.int32)
    hot_hit = (own_slots[:, None] == hot_ids[None, :]).astype(jnp.float32)
    grad_table = jnp.dot(hot_hit.T, flat_grad, precision=lax.Precision.HIGHEST)
    grad_table = lax.psum(grad_table.astype(jnp.bfloat16), "expert").astype(jnp.float32)
    hot_flag = jnp.sum(hot_hit, axis=1, keepdims=True)
    grad_flat = (
        jnp.dot(hot_hit, grad_table, precision=lax.Precision.HIGHEST) + (1.0 - hot_flag) * flat_grad
    )
    grad_total = grad_flat.reshape(local_grad.shape)
    new_first = beta_one * first_moment.astype(jnp.float32) + (1.0 - beta_one) * grad_total
    new_second = (
        beta_two * second_moment.astype(jnp.float32) + (1.0 - beta_two) * grad_total * grad_total
    )
    update = (
        new_first / correct_one / (jnp.sqrt(new_second / correct_two) + epsilon)
        + decay_rate * master
    )
    new_master = master - learn_rate * update
    return (
        hidden_grad[None, None],
        gate_grad,
        new_master,
        new_first.astype(jnp.bfloat16),
        new_second.astype(jnp.bfloat16),
    )


def solution(mesh):
    placed = (
        P(("dp", "expert"), None),
        P(("dp", "expert"), None),
        P(("dp", "expert"), None),
        P(("dp", "expert"), None),
        P(),
        P("dp", "expert", None, None, None, None),
        P("expert", "dp", None),
        P("expert", "dp", None),
        P("expert", "dp", None),
    )
    return jax.shard_map(
        on_device,
        mesh=mesh,
        in_specs=placed,
        out_specs=(
            P("dp", "expert", None, None, None, None),
            P(("dp", "expert"), None),
            P("expert", "dp", None),
            P("expert", "dp", None),
            P("expert", "dp", None),
        ),
        check_vma=False,
    )
```

profile of v0, /device:TPU:0, one launch (start us, length us, event | category | flops | bytes accessed | tf_op | source)
XLA Modules:
  0.0 714.3 jit_solution(12288854935570546787)
XLA Ops:
  7.2 0.8 copy.62
  8.1 0.9 convert_reduce_fusion
  9.0 0.7 fusion.15
  9.7 0.8 copy.63
  10.7 0.7 select_reduce_fusion
  11.5 1.2 reduce-window.6
  13.0 0.7 convert_element_type.67
  14.0 3.8 scatter_custom_fusion
  17.8 0.7 reshape.109
  18.4 7.3 %all-to-all-start = ((bf16[8,2,48]{2,1,0:T(2,128)(2,1)}), bf16[8,2,48]{2,1,0:T(2,128)(2,1)S(1)}, u32[]{:S(2)}, u32[]{:S(2)}) async-start(bf16[8,2,48]{2,1,0:T(2,128)(2,1)} %reshape.109), calls=%async_computation | async-start | bytes 8192 | tf_op jit(solution)/shard_map/all_to_all | solution.py:66
  25.7 4.0 broadcast_in_dim.56
  29.7 6.7 reshape.137
  36.4 10.3 %scatter_custom_fusion.1 = bf16[768,3584]{1,0:T(8,128)(2,1)} fusion(s32[512]{0:T(512)S(1)} %bitcast.79, bf16[512,3584]{1,0:T(8,128)(2,1)} %reshape.137, bf16[]{:T(256)} %constant.18.clone.1), kind=kCustom, calls=%fused_computation.23 | custom fusion | bytes 5505536 | tf_op jit(solution)/shard_map/scatter | solution.py:51
  46.7 6.0 all-to-all-start.1
  53.0 120.5 %all-to-all-done.1 = bf16[8,2,48,3584]{3,2,1,0:T(8,128)(2,1)} async-done(((bf16[8,2,48,3584]{3,2,1,0:T(8,128)(2,1)}), bf16[8,2,48,3584]{3,2,1,0:T(8,128)(2,1)}, u32[]{:S(2)}, u32[]{:S(2)}) %all-to-all-start.1) | async-done | bytes 5505056 | tf_op jit(solution)/shard_map/all_to_all | solution.py:59
  173.5 14.1 %fusion = bf16[1024,2,3584]{0,2,1:T(8,128)(2,1)} fusion(bf16[8,2,48,3584]{3,2,1,0:T(8,128)(2,1)} %all-to-all-done.1, f32[8,2,48]{2,1,0:T(2,128)S(1)} %convert_element_type.69, bf16[1,1,8,2,48,1024]{5,4,3,2,1,0:T(8,128)(2,1)S(1)} %copy-done.2), kind=kOutput, calls=%fused_computation.6 | convolution fusion | flops 5652742144 | bytes 21761024 | tf_op jit(solution)/shard_map/qlch,qlcd->hld/dot_general | solution.py:89
  188.3 111.4 %reduce-scatter.2.cloned.1.call-done = bf16[256,2,3584]{0,2,1:T(8,128)(2,1)} async-done(((bf16[1024,2,3584]{0,2,1:T(8,128)(2,1)}), bf16[256,2,3584]{0,2,1:T(8,128)(2,1)}) %reduce-scatter.2.cloned.1.call-update) | async-done | bytes 3670032 | tf_op jit(solution)/shard_map/reduce_scatter | solution.py:88
  299.7 5.9 copy.71
  305.7 5.8 copy.77
  311.5 1.8 copy-done
  313.3 6.9 convolution_convert_fusion
  320.8 241.2 %all-reduce.2.cloned.1.call-done = bf16[3,917504]{1,0:T(4,128)(2,1)} async-done(((bf16[3,917504]{1,0:T(4,128)(2,1)}), bf16[3,917504]{1,0:T(4,128)(2,1)}) %all-reduce.2.cloned.1.call-update) | async-done | bytes 5505040 | tf_op jit(solution)/shard_map/psum | solution.py:102
  562.0 7.4 %convolution_add_fusion = f32[2,917504]{1,0:T(2,128)S(1)} fusion(bf16[3,917504]{1,0:T(4,128)(2,1)} %all-reduce.2.cloned.1.call-done, bf16[2,917504]{1,0:T(2,128)(2,1)} %bitcast.76, f32[2]{0:T(128)S(1)} %broadcast_subtract_fusion, s32[2]{0:T(128)S(1)} %dynamic_slice.3), kind=kOutput, calls=%fused_computation.4 | convolution fusion | flops 16515078 | bytes 16515088 | tf_op jit(solution)/shard_map/dot_general | solution.py:105
  569.5 18.1 %fusion.8 = (bf16[2,256,3584]{2,1,0:T(8,128)(2,1)}, f32[2,256,3584]{2,1,0:T(8,128)}, bf16[2,256,3584]{2,1,0:T(8,128)(2,1)}, bf16[2,256,3584]{2,1,0:T(8,128)(2,1)}) fusion(f32[1,2,256,3584]{3,1,2,0:T(2,128)S(1)} %bitcast.73, bf16[2,256,3584]{2,1,0:T(8,128)(2,1)} %param.17, f32[2,256,3584]{2,1,0:T(8,128)} %param.15, bf16[2,256,3584]{2,1,0:T(8,128)(2,1)} %param.16), kind=kLoop, calls=%fused_computation.18 | loop fusion | flops 36700160 | bytes 40370176 | tf_op jit(solution)/shard_map/convert_element_type | solution.py:122
  587.6 93.2 %all-gather.2.cloned.1.call-done = bf16[2,1024,3584]{2,1,0:T(8,128)(2,1)} async-done(((bf16[2,256,3584]{2,1,0:T(8,128)(2,1)}), bf16[2,1024,3584]{2,1,0:T(8,128)(2,1)}) %all-gather.2.cloned.1.call-update) | async-done | bytes 14680080 | tf_op jit(solution)/shard_map/all_gather | solution.py:79
  680.8 11.1 %fusion.10 = (f32[8,2,48]{2,0,1:T(8,128)S(1)}, bf16[1,1,8,2,48,1024]{5,4,2,3,1,0:T(8,128)(2,1)S(1)}) fusion(bf16[1,1,8,2,48,1024]{5,4,3,2,1,0:T(8,128)(2,1)} %param.14, f32[8,2,48]{2,0,1:T(8,128)S(1)} %copy.66, bf16[2,1024,3584]{2,1,0:T(8,128)(2,1)} %all-gather.2.cloned.1.call-done, bf16[8,2,48,3584]{3,2,1,0:T(8,128)(2,1)} %all-to-all-done.1), kind=kOutput, calls=%fused_computation.22 | convolution fusion | flops 5641075712 | bytes 23336960 | tf_op jit(solution)/shard_map/qlcd,lhd->qlch/dot_general | solution.py:76
  692.0 0.6 copy.69
  692.6 5.5 all-to-all-start.2
  698.1 1.3 copy.72
  699.4 5.2 all-to-all-done.2
  704.7 2.3 gather_fusion
  707.1 0.7 copy.73
  (32 shorter events, 2.7 us)
Async XLA Ops:
  18.4 28.2 %all-to-all-start = ((bf16[8,2,48]{2,1,0:T(2,128)(2,1)}), bf16[8,2,48]{2,1,0:T(2,128)(2,1)S(1)}, u32[]{:S(2)}, u32[]{:S(2)}) async-start(bf16[8,2,48]{2,1,0:T(2,128)(2,1)} %reshape.109), calls=%async_computation | async-start | bytes 8192 | tf_op jit(solution)/shard_map/all_to_all | solution.py:66
  36.4 137.1 %copy-start.2 = (bf16[1,1,8,2,48,1024]{5,4,3,2,1,0:T(8,128)(2,1)S(1)}, bf16[1,1,8,2,48,1024]{5,4,3,2,1,0:T(8,128)(2,1)}, u32[]{:S(2)}) copy-start(bf16[1,1,8,2,48,1024]{5,4,3,2,1,0:T(8,128)(2,1)} %param.14) | copy-start | bytes 4718596
  46.7 126.8 %all-to-all-start.1 = ((bf16[8,2,48,3584]{3,2,1,0:T(8,128)(2,1)}), bf16[8,2,48,3584]{3,2,1,0:T(8,128)(2,1)}, u32[]{:S(2)}, u32[]{:S(2)}) async-start(bf16[8,2,48,3584]{3,2,1,0:T(8,128)(2,1)} %bitcast.71), calls=%async_computation.1 | async-start | bytes 11010048 | tf_op jit(solution)/shard_map/all_to_all | solution.py:59
  52.7 247.0 %reduce-scatter.2.cloned.1.call-start = ((), (), s32[]{:S(2)}) async-start(), calls=%async_computation.5 | async-start | bytes 18350080 | tf_op jit(solution)/shard_map/reduce_scatter | solution.py:88
  187.5 0.7 copy-start.1
  187.6 374.4 %all-reduce.2.cloned.1.call-start = ((), (), s32[]{:S(2)}) async-start(), calls=%async_computation.6 | async-start | bytes 14680064 | tf_op jit(solution)/shard_map/psum | solution.py:102
  311.5 1.8 copy-start
  320.3 360.5 %all-gather.2.cloned.1.call-start = ((), (), s32[]{:S(2)}) async-start(), calls=%async_computation.4 | async-start | bytes 18350080 | tf_op jit(solution)/shard_map/all_gather | solution.py:79
  692.6 12.0 %all-to-all-start.2 = ((f32[8,2,48]{2,1,0:T(2,128)}), f32[8,2,48]{2,1,0:T(2,128)S(1)}, u32[]{:S(2)}, u32[]{:S(2)}) async-start(f32[8,2,48]{2,1,0:T(2,128)} %copy.69), calls=%async_computation.2 | async-start | bytes 16384 | tf_op jit(solution)/shard_map/all_to_all | solution.py:85
Sparse Core Ops, SparseCore 0:
  187.7 111.9 reduce-scatter.1
  320.4 241.5 all-reduce.1
  587.7 93.0 all-gather.1
where the time goes:
time: 715 us; the launch traced here: 714 us
  waiting for transfers between devices  572 us (80%)
  local copies, waits for them, and re-layouts  47 us (7%)
  matrix products  39.6 us (6%)
  other arithmetic  22.8 us (3%)
  starting transfers between devices  19.4 us (3%)
  between operations  13.9 us (2%)
    psum x1, waiting for transfers between devices, on_device(): lax.psum(grad_table.astype(jnp.bfloat16), 'expert').astype(jnp.float32)  241 us
    all_to_all x1, waiting for transfers between devices, on_device(): lax.all_to_all(send_rows.reshape(dev_count, slot_dev, capacity, feature_c...  121 us
    reduce_scatter x1, waiting for transfers between devices, on_device(): lax.psum_scatter(jnp.einsum('qlch,qlcd->hld', hidden, scaled, preferred_e...  111 us
    all_gather x1, waiting for transfers between devices, on_device(): lax.all_gather(weights, 'dp', axis=1, tiled=True)  93.2 us
    convert_element_type x1, other arithmetic, on_device(): new_second.astype(jnp.bfloat16)  18.1 us
  transfers between devices with their start and end apart: 6, of which 5 were waited for; matrix products, arithmetic and copies ran while one was open for 3% of the time, Pallas kernels for 0%

commit v1 on v0

v1 whole, which is shorter than its diff:
```python
import jax
import jax.numpy as jnp
from jax import lax
from jax.experimental import pallas as pl
from jax.experimental.pallas import tpu as pltpu
from jax.sharding import PartitionSpec as P

HOT = 3
CORES = 2

beta_one = 0.9
beta_two = 0.95
learn_rate = 0.00022
decay_rate = 0.1
epsilon = 1e-08
correct_one = 0.6513215599
correct_two = 0.4012630607

bf16, f32 = jnp.bfloat16, jnp.float32


def matmul(spec, left, right):
    return jnp.einsum(spec, left, right, preferred_element_type=f32)


def dot(left, right, left_dim, right_dim, precision=None):
    return lax.dot_general(
        left,
        right,
        (((left_dim,), (right_dim,)), ((), ())),
        precision=precision,
        preferred_element_type=f32,
    )


def kernel_params():
    return pltpu.CompilerParams(vmem_limit_bytes=60 * 1024 * 1024)


def adam(grad, master, first, second):
    new_first = beta_one * first.astype(f32) + (1.0 - beta_one) * grad
    new_second = beta_two * second.astype(f32) + (1.0 - beta_two) * grad * grad
    update = (new_first * (1.0 / correct_one)) / (
        jnp.sqrt(new_second * (1.0 / correct_two)) + epsilon
    ) + decay_rate * master
    return master - learn_rate * update, new_first.astype(bf16), new_second.astype(bf16)


def gate(values, waits):
    def body(*refs):
        pass

    return pl.pallas_call(
        body,
        out_shape=[jax.ShapeDtypeStruct(v.shape, v.dtype) for v in values],
        in_specs=[pl.BlockSpec(memory_space=pl.ANY)] * (len(values) + len(waits)),
        out_specs=[pl.BlockSpec(memory_space=pl.ANY)] * len(values),
        input_output_aliases={i: i for i in range(len(values))},
        cost_estimate=light(),
    )(*values, *waits)


def column_hits(columns, gates, capacity):
    by_token = dot(columns, gates, 1, 1)
    live = by_token > 0
    tokens = gates.shape[0]
    row = lax.broadcasted_iota(jnp.int32, (tokens, tokens), 0)
    col = lax.broadcasted_iota(jnp.int32, (tokens, tokens), 1)
    earlier = jnp.where(row < col, 1.0, 0.0).astype(bf16)
    spot = dot(jnp.where(live, 1.0, 0.0).astype(bf16), earlier, 1, 0).astype(jnp.int32)
    spot = jnp.where(live, spot, -1)
    places = lax.broadcasted_iota(jnp.int32, (capacity, tokens), 0)

    def hit(at):
        return jnp.where(spot[at : at + 1] == places, 1.0, 0.0)

    return by_token, hit


def light():
    return pl.CostEstimate(flops=1, bytes_accessed=1, transcendentals=0)


def route_tables(columns, gates, slot_dev, capacity):
    peers, tokens, slots = gates[0].shape

    def body(columns_ref, ng_ref, fg_ref, hit_ref, back_ref, scale_ref):
        for at in range(4):
            plane, peer = at // 2, at % 2
            source_gates = (ng_ref, fg_ref)[plane][peer]
            by_token, hit = column_hits(columns_ref[...], source_gates, capacity)
            for l in range(slot_dev):
                hits = hit(l)
                hit_ref[plane, peer, l] = hits.astype(bf16)
                back_ref[plane, peer, l] = (hits * by_token[l : l + 1]).astype(bf16)
                at_expert = slot_dev + l
                scale = hit(at_expert) * by_token[at_expert : at_expert + 1]
                scale_ref[plane, peer, l] = scale.astype(bf16)

    gate_spec = pl.BlockSpec((2, tokens, slots), lambda q: (q, 0, 0))
    hit_spec = pl.BlockSpec((2, 2, slot_dev, capacity, tokens), lambda q: (0, q, 0, 0, 0))
    hit_shape = jax.ShapeDtypeStruct((2, peers, slot_dev, capacity, tokens), bf16)
    return pl.pallas_call(
        body,
        grid=(peers // 2,),
        out_shape=[hit_shape] * 3,
        in_specs=[pl.BlockSpec(columns.shape, lambda q: (0, 0)), gate_spec, gate_spec],
        out_specs=[hit_spec] * 3,
        compiler_params=kernel_params(),
        cost_estimate=light(),
    )(columns, *gates)


def add_planes(sums, wait):
    count, slot_dev, tokens = sums.shape

    def body(sums_ref, wait_ref, out_ref):
        out_ref[...] = sums_ref[: count // 2] + sums_ref[count // 2 :]

    return pl.pallas_call(
        body,
        in_specs=[
            pl.BlockSpec(memory_space=pltpu.VMEM),
            pl.BlockSpec(memory_space=pl.ANY),
        ],
        out_shape=jax.ShapeDtypeStruct((count // 2, slot_dev, tokens), f32),
        cost_estimate=light(),
    )(sums, wait)


def cast_weight(master, waits):
    slot_dev, shard_rows, features = master.shape
    block = (1, shard_rows, features)

    def body(*refs):
        refs[-1][...] = refs[0][...].astype(bf16)

    return pl.pallas_call(
        body,
        grid=(slot_dev,),
        in_specs=[pl.BlockSpec(block, lambda l: (l, 0, 0))]
        + [pl.BlockSpec(memory_space=pl.ANY)] * len(waits),
        out_specs=pl.BlockSpec(block, lambda l: (l, 0, 0)),
        out_shape=jax.ShapeDtypeStruct(master.shape, bf16),
        compiler_params=kernel_params(),
        cost_estimate=light(),
    )(master, *waits)


def split_hidden(plane, hidden):
    devs, slot_dev, capacity, width = hidden.shape
    block = (devs // 2, slot_dev, capacity, width // 2)

    def body(plane_ref, own_ref, other_ref, own_out, other_out):
        own_out[...] = own_ref[...]
        other_out[...] = other_ref[...]

    out_spec = pl.BlockSpec(block, lambda i, plane: (i, 0, 0, 0))
    shape = jax.ShapeDtypeStruct((devs, slot_dev, capacity, width // 2), bf16)
    return pl.pallas_call(
        body,
        grid_spec=pltpu.PrefetchScalarGridSpec(
            num_scalar_prefetch=1,
            grid=(2,),
            in_specs=[
                pl.BlockSpec(block, lambda i, plane: (i, 0, 0, plane[0])),
                pl.BlockSpec(block, lambda i, plane: (i, 0, 0, 1 - plane[0])),
            ],
            out_specs=[out_spec, out_spec],
        ),
        out_shape=[shape, shape],
        compiler_params=kernel_params(),
        cost_estimate=light(),
    )(plane, hidden, hidden)


def hot_part(columns, gates, rows, pairs):
    slots, capacity, width = rows.shape
    planes = 2

    def body(columns_ref, gates_ref, rows_ref, pairs_ref, out_ref):
        _, hit = column_hits(columns_ref[...], gates_ref[...], capacity)
        slots_of = jnp.concatenate([hit(s) for s in range(slots)], axis=0).astype(bf16)
        hots = jnp.concatenate([hit(slots + j) for j in range(HOT)], axis=0).astype(bf16)
        moved = (dot(hots, slots_of, 1, 1) * pairs_ref[...]).astype(bf16)
        table = dot(moved, rows_ref[...].reshape(slots * capacity, width), 1, 0).astype(bf16)
        for x in range(planes):
            part = table[:, x * (width // planes) : (x + 1) * (width // planes)]
            out_ref[x] = part.reshape(HOT, capacity, width // planes)

    return pl.pallas_call(
        body,
        out_shape=jax.ShapeDtypeStruct((planes, HOT, capacity, width // planes), bf16),
        compiler_params=kernel_params(),
        cost_estimate=light(),
    )(columns, gates, rows, pairs)


def whole_spec(shape):
    return pl.BlockSpec(shape, lambda *_: (0,) * len(shape))


def project_set(sources, peers, core, pieces, weights, hits, backs, rows, keep):
    devs, slot_dev, capacity, plane_rows = rows[0].shape
    tok_rows = hits.shape[-1]
    shard_rows, features = weights[0].shape[1:]
    total = len(sources) * tok_rows
    count = len(pieces)
    far_count = sum(plane for plane, _ in sources)
    counts = (len(sources) - far_count, far_count)

    def body(peers_ref, core_ref, *refs):
        token_refs = refs[:count]
        own_ref, other_ref, hit_ref, scatter_ref, nr_ref, fr_ref = refs[count : count + 6]
        near_ref, far_ref, sums_ref = refs[count + 6 : count + 9]
        weight_scr, group_ref = refs[-1 if keep else -2], refs[-2 if keep else -1]
        slot = pl.program_id(0)

        @pl.when(slot == 0)
        def _():
            start = 0
            for ref in token_refs:
                group_ref[start : start + ref.shape[0], :] = ref[...]
                start += ref.shape[0]

        sums = [0.0] * len(sources)
        scatters = [scatter_ref[p, peers_ref[k], slot].astype(f32) for p, k in sources]
        row_gates = [jnp.sum(scatter, axis=1, keepdims=True) for scatter in scatters]
        weight_scr[:shard_rows] = own_ref[0]
        weight_scr[shard_rows:] = other_ref[0]
        both = dot(group_ref[...], weight_scr[...], 1, 1).astype(bf16)
        for j in range(CORES):
            half = pl.multiple_of((core_ref[0] ^ j) * shard_rows, shard_rows)
            projected = both[:, j * shard_rows : (j + 1) * shard_rows]
            filled = [0, 0]
            for at, (plane, index) in enumerate(sources):
                peer = peers_ref[index]
                mine = projected[at * tok_rows : (at + 1) * tok_rows]
                picked = dot(hit_ref[plane, peer, slot], mine, 1, 0)
                saved = (nr_ref, fr_ref)[plane][peer, slot, :, pl.ds(half, shard_rows)]
                sums[at] = sums[at] + jnp.sum(saved.astype(f32) * picked, axis=1, keepdims=True)
                out_ref = (near_ref, far_ref)[plane]
                back = (row_gates[at] * picked).astype(bf16)
                out_ref[filled[plane], 0, :, pl.ds(half, shard_rows)] = back
                filled[plane] += 1
        for at, (plane, index) in enumerate(sources):
            hits = hit_ref[plane, peers_ref[index], slot].astype(f32)
            sums_ref[0, at : at + 1] = jnp.sum(hits * sums[at], axis=0, keepdims=True)

    def back_spec(number):
        return pl.BlockSpec((number, 1, capacity, plane_rows), lambda l, p, c: (0, l, 0, 0))

    def back_shape(number):
        return jax.ShapeDtypeStruct((number, slot_dev, capacity, plane_rows), bf16)

    weight_spec = pl.BlockSpec((1, shard_rows, features), lambda l, p, c: (l, 0, 0))
    return pl.pallas_call(
        body,
        grid_spec=pltpu.PrefetchScalarGridSpec(
            num_scalar_prefetch=2,
            grid=(slot_dev,),
            in_specs=[whole_spec(t.shape) for t in pieces]
            + [
                weight_spec,
                weight_spec,
                whole_spec(hits.shape),
                whole_spec(backs.shape),
                whole_spec(rows[0].shape),
                whole_spec(rows[1].shape),
            ],
            out_specs=[
                back_spec(counts[0]),
                back_spec(counts[1]),
                pl.BlockSpec((1, len(sources), tok_rows), lambda l, p, c: (l, 0, 0)),
            ]
            + ([whole_spec((total, features))] if keep else []),
            scratch_shapes=[pltpu.VMEM((CORES * shard_rows, features), bf16)]
            + ([] if keep else [pltpu.VMEM((total, features), bf16)]),
        ),
        out_shape=[
            back_shape(counts[0]),
            back_shape(counts[1]),
            jax.ShapeDtypeStruct((slot_dev, len(sources), tok_rows), f32),
        ]
        + ([jax.ShapeDtypeStruct((total, features), bf16)] if keep else []),
        compiler_params=kernel_params(),
        cost_estimate=pl.CostEstimate(
            flops=2 * total * features * slot_dev * plane_rows,
            bytes_accessed=2 * features * (2 * total + slot_dev * plane_rows),
            transcendentals=0,
        ),
    )(peers, core, *pieces, *weights, hits, backs, *rows)


def hidden_parts(peers, plane, near, far, near_order, far_order):
    slot_dev, capacity, plane_rows = near[0].shape[1:]
    devs = peers.shape[0]

    def body(peers_ref, plane_ref, *refs):
        out_ref = refs[-1]
        for arrays, order, flip in (
            (refs[: len(near)], near_order, 0),
            (refs[len(near) : -1], far_order, 1),
        ):
            half = pl.multiple_of((plane_ref[0] ^ flip) * plane_rows, plane_rows)
            flat = [ref.at[i] for ref in arrays for i in range(ref.shape[0])]
            for ref, index in zip(flat, order):
                out_ref[peers_ref[index], :, :, pl.ds(half, plane_rows)] = ref[...]

    shape = (devs, slot_dev, capacity, 2 * plane_rows)
    return pl.pallas_call(
        body,
        grid_spec=pltpu.PrefetchScalarGridSpec(
            num_scalar_prefetch=2,
            grid=(1,),
            in_specs=[whole_spec(v.shape) for v in (*near, *far)],
            out_specs=whole_spec(shape),
        ),
        out_shape=jax.ShapeDtypeStruct(shape, bf16),
        compiler_params=kernel_params(),
        cost_estimate=light(),
    )(peers, plane, *near, *far)


def scaled_rows(places, own_expert, scales, rows, table):
    slot_dev, capacity, plane_rows = rows[0].shape[1:]
    tok_rows = scales.shape[-1]
    width = slot_dev * plane_rows
    sources = places.shape[0]

    def body(places_ref, expert_ref, scale_ref, nr_ref, fr_ref, table_ref, out_ref):
        group = pl.program_id(0)
        for at in range(4):
            plane, peer = places_ref[4 * group + at, 0], places_ref[4 * group + at, 1]
            for l in range(slot_dev):
                expert = expert_ref[l]
                hot = table_ref[peer, plane, jnp.minimum(expert, HOT - 1)]
                own = jnp.where(plane == 0, nr_ref[peer, l], fr_ref[peer, l])
                picked = jnp.where(expert < HOT, hot, own)
                part = dot(picked, scale_ref[plane, peer, l], 0, 0).astype(bf16)
                out_ref[
                    l * plane_rows : (l + 1) * plane_rows, at * tok_rows : (at + 1) * tok_rows
                ] = part

    return pl.pallas_call(
        body,
        grid_spec=pltpu.PrefetchScalarGridSpec(
            num_scalar_prefetch=2,
            grid=(sources // 4,),
            in_specs=[
                whole_spec(scales.shape),
                whole_spec(rows[0].shape),
                whole_spec(rows[1].shape),
                whole_spec(table.shape),
            ],
            out_specs=pl.BlockSpec((width, 4 * tok_rows), lambda g, p, e: (0, g)),
        ),
        out_shape=jax.ShapeDtypeStruct((width, sources * tok_rows), bf16),
        compiler_params=kernel_params(),
        cost_estimate=light(),
    )(places, own_expert, scales, *rows, table)


def early_grad(groups, scaled):
    width, total = scaled.shape
    features = groups[0].shape[1]
    tile = 512 if features % 512 == 0 else features

    def body(*refs):
        scaled_ref, out_ref = refs[-2:]
        grad, start = 0.0, 0
        for ref in refs[:-2]:
            depth = ref.shape[0]
            grad = grad + dot(scaled_ref[:, start : start + depth], ref[...], 1, 0)
            start += depth
        out_ref[...] = grad.astype(bf16)

    return pl.pallas_call(
        body,
        grid=(features // tile,),
        in_specs=[pl.BlockSpec((g.shape[0], tile), lambda n: (0, n)) for g in groups]
        + [whole_spec(scaled.shape)],
        out_specs=pl.BlockSpec((width, tile), lambda n: (0, n)),
        out_shape=jax.ShapeDtypeStruct((width, features), bf16),
        compiler_params=kernel_params(),
        cost_estimate=pl.CostEstimate(
            flops=2 * total * features * width,
            bytes_accessed=2 * features * (total + width),
            transcendentals=0,
        ),
    )(*groups, scaled)


def last_grad(chunk, pieces, scaled, early, state=None):
    slot_dev, _, shard_rows, columns = scaled.shape
    total = sum(piece.shape[0] for piece in pieces)
    part = columns // total - 1
    features = pieces[0].shape[1]
    tile = 896 if state is None else 512
    tile = tile if features % tile == 0 else features
    count = len(pieces)

    def body(chunk_ref, *refs):
        scaled_ref, early_ref = refs[count : count + 2]
        last_ref = refs[-1]
        start = 0
        for ref in refs[:count]:
            last_ref[start : start + ref.shape[0], :] = ref[...]
            start += ref.shape[0]
        for l in range(slot_dev):
            grad = dot(scaled_ref[l, 0], last_ref[...], 1, 0) + early_ref[l, 0].astype(f32)
            if state is None:
                refs[count + 2][l] = grad.astype(bf16)
            else:
                given, master, first, second, o_master, o_first, o_second = refs[count + 2 : -1]
                grad = grad + given[l].astype(f32)
                o_master[l], o_first[l], o_second[l] = adam(grad, master[l], first[l], second[l])

    shard = pl.BlockSpec((slot_dev, shard_rows, tile), lambda n, chunk: (0, 0, n))
    shape = (slot_dev, shard_rows, features)
    outs = [bf16] if state is None else [f32, bf16, bf16]
    extra = () if state is None else state
    return pl.pallas_call(
        body,
        grid_spec=pltpu.PrefetchScalarGridSpec(
            num_scalar_prefetch=1,
            grid=(features // tile,),
            in_specs=[pl.BlockSpec((t.shape[0], tile), lambda n, chunk: (0, n)) for t in pieces]
            + [
                pl.BlockSpec(
                    (slot_dev, 1, shard_rows, total), lambda n, chunk: (0, chunk[0], 0, part)
                ),
                pl.BlockSpec(
                    (slot_dev, 1, shard_rows, tile), lambda n, chunk: (0, chunk[0], 0, n)
                ),
            ]
            + [shard] * len(extra),
            out_specs=[shard] * len(outs),
            scratch_shapes=[pltpu.VMEM((total, tile), bf16)],
        ),
        out_shape=[jax.ShapeDtypeStruct(shape, kind) for kind in outs],
        compiler_params=kernel_params(),
        cost_estimate=light()
        if state is None
        else pl.CostEstimate(
            flops=2 * total * features * slot_dev * shard_rows,
            bytes_accessed=2 * total * features + 24 * slot_dev * shard_rows * features,
            transcendentals=0,
        ),
    )(chunk, *pieces, scaled, early, *extra)


def on_device(
    grad_out,
    gate_probs,
    expert_route,
    replica_pick,
    slot_expert,
    saved_hidden,
    master,
    first_moment,
    second_moment,
):
    dp_count = lax.axis_size("dp")
    dev_count = lax.axis_size("expert")
    planes = dp_count // CORES
    slot_count = slot_expert.shape[0]
    slot_dev = slot_count // dev_count
    capacity, hidden_count = saved_hidden.shape[4:]
    tok_rows, top_count = gate_probs.shape
    feature_count = grad_out.shape[1]
    shard_rows = master.shape[1]
    plane_rows = CORES * shard_rows
    width = slot_dev * plane_rows
    dp_index = lax.axis_index("dp")
    dev_index = lax.axis_index("expert")
    plane, core = dp_index // CORES, dp_index % CORES

    def from_plane(value, shift):
        pairs = [(i, (i + shift * CORES) % dp_count) for i in range(dp_count)]
        return lax.ppermute(value, "dp", pairs)

    def from_sibling(value):
        return lax.ppermute(value, "dp", [(i, i ^ 1) for i in range(dp_count)])

    def from_peer(value, bits):
        return lax.ppermute(value, "expert", [(i, i ^ bits) for i in range(dev_count)])

    slot_ids = jnp.arange(slot_count, dtype=jnp.int32)
    same_expert = slot_expert[:, None] == slot_expert[None, :]
    slot_rank = jnp.sum(same_expert & (slot_ids[None, :] < slot_ids[:, None]), axis=1)
    host_mask = slot_expert[None, None, :] == expert_route[:, :, None]
    copy_count = jnp.sum(host_mask.astype(jnp.int32), axis=2)
    chosen = host_mask & (slot_rank == (replica_pick % copy_count)[:, :, None])
    slot_gates = jnp.sum(
        jnp.where(chosen, gate_probs.astype(bf16)[:, :, None], 0).astype(f32), axis=1
    ).astype(bf16)
    copies = jnp.broadcast_to(slot_gates[None], (dp_count * dev_count, tok_rows, slot_count))
    all_gates = lax.all_to_all(copies, ("dp", "expert"), split_axis=0, concat_axis=0, tiled=True)
    all_gates = all_gates.reshape(planes, CORES, dev_count, tok_rows, slot_count)
    all_gates = lax.dynamic_index_in_dim(all_gates, core, 1, keepdims=False)

    first_slot = dev_index * slot_dev
    own_ids = first_slot + jnp.arange(slot_dev, dtype=jnp.int32)
    own_expert = lax.dynamic_slice_in_dim(slot_expert, first_slot, slot_dev)
    hot_ids = jnp.arange(HOT, dtype=jnp.int32)
    columns = jnp.concatenate(
        [
            slot_ids[:, None] == own_ids[None, :],
            slot_expert[:, None] == own_expert[None, :],
            slot_expert[:, None] == hot_ids[None, :],
        ],
        axis=1,
    ).astype(bf16)
    hot_own = (own_expert[:, None] == hot_ids[None, :]).astype(bf16)

    def by_plane(values):
        if planes == 2:
            flip = plane == 1
            return [jnp.where(flip, values[1 - i], values[i]) for i in range(2)]
        stacked = jnp.stack(values)
        order = (plane - jnp.arange(planes)) % planes
        return list(jnp.take(stacked, order, axis=0))

    def finish(hidden_grad, gate_sums, state):
        by_slot = gate_sums.transpose(1, 0, 2).reshape(tok_rows, slot_count)
        gate_grad = jnp.sum(jnp.where(chosen, by_slot[:, None, :], 0.0), axis=2)
        return (hidden_grad[None, None], gate_grad, *state)

    if planes == 2 and dev_count == 8:
        columns = jnp.pad(columns, ((0, 0), (0, 16 - columns.shape[1]))).T
        gates = [
            lax.dynamic_index_in_dim(all_gates, (plane + i) % planes, 0, keepdims=False)
            for i in range(planes)
        ]
        ends = dev_index // 2
        inner = (ends == 1) | (ends == 2)

        def arrival(index):
            return jnp.where(inner & (index >= 4), index ^ 2, index)

        everyone = jnp.arange(dev_count, dtype=jnp.int32)
        peers = dev_index ^ arrival(everyone)
        position = arrival(dev_index ^ everyone)

        def along(value, moves):
            pairs = [(2 * i + y, 2 * j + y) for i, j in moves for y in range(2)]
            return lax.ppermute(value, "expert", pairs)

        across, outward = [(1, 2), (2, 1)], [(1, 0), (2, 3)]
        middle = tok_rows // 2

        pair = from_peer(grad_out, 2)
        mid = along(grad_out, across)
        side_0 = from_peer(grad_out, 1)
        far_0 = from_plane(grad_out, 1)
        plane_at = plane.astype(jnp.int32).reshape(1)
        near_rows, far_rows = split_hidden(plane_at, saved_hidden[0, 0])
        rows = (near_rows, from_plane(far_rows, 1))
        raw = lax.all_to_all(saved_hidden[0, 0], "expert", split_axis=0, concat_axis=0, tiled=True)
        raw = raw.reshape(slot_count, capacity, hidden_count)
        diag_0 = from_peer(far_0, 1)
        pair, mid, raw = gate((pair, mid, raw), (side_0, rows[1], diag_0, slot_gates))

        slot_hits, slot_backs, scales = route_tables(columns, gates, slot_dev, capacity)
        core_at = core.astype(jnp.int32).reshape(1)

        def project(sources, pieces, keep=True):
            return project_set(
                sources, peers, core_at, pieces, weights, slot_hits, slot_backs, rows, keep
            )

        every = jnp.concatenate([slot_ids, hot_ids])
        is_hot = jnp.arange(every.shape[0]) >= slot_count
        chooser = jnp.where(
            is_hot[:, None], slot_expert[None, :] == every[:, None], slot_ids == every[:, None]
        )
        chooser = jnp.pad(chooser.astype(bf16), ((0, -every.shape[0] % 16), (0, 0)))
        pairs = (hot_ids[:, None] == slot_expert[None, :]).astype(f32)
        pairs = jnp.repeat(jnp.repeat(pairs, capacity, axis=0), capacity, axis=1)

        moved_mid = along(mid, outward)
        moved_pair = along(pair, across)
        side_1, far_1 = from_peer(pair, 1), from_plane(pair, 1)
        table = hot_part(chooser, slot_gates, raw, pairs)
        table = [
            lax.dynamic_index_in_dim(table, (plane + i) % planes, 0, keepdims=False)
            for i in range(planes)
        ]
        table_far = from_plane(table[1], 1)

        mid, moved_mid, moved_pair, side_1, far_1, table_far = gate(
            (mid, moved_mid, moved_pair, side_1, far_1, table_far), (scales,)
        )
        own_weight = cast_weight(master, (moved_mid,))
        weights = (own_weight, from_sibling(own_weight))
        second = jnp.where(inner, mid, moved_mid)
        last = along(moved_pair, outward)
        side_2, far_2 = from_peer(second, 1), from_plane(second, 1)
        diag_1 = from_plane(side_1, 1)
        table = jnp.stack([table[0], table_far])
        table_side = from_peer(table, 1)
        order_a = ((0, 0), (0, 2), (1, 0), (0, 1), (0, 4), (0, 3), (1, 2))
        set_a = project(order_a, (grad_out, pair, far_0, side_0, second, side_1, far_1))
        (table_side,) = gate((table_side,), (last,))
        even = dev_index % 2 == 0
        table = jnp.stack([jnp.where(even, table, table_side), jnp.where(even, table_side, table)])
        lines = [list(range(y, dev_count, 2)) for y in range(2)]
        table = lax.all_gather(table[None], "expert", axis_index_groups=lines, tiled=True)
        table = table.reshape(dev_count, *table.shape[2:])

        moved_pair, last, side_2, far_2 = gate(
            (moved_pair, last, side_2, far_2), (diag_1, set_a[2])
        )
        third = jnp.where(inner, moved_pair, last)
        side_3, far_3 = from_peer(third, 1), from_plane(third, 1)
        order_b = ((1, 1), (1, 3), (1, 4), (0, 5), (0, 6))
        set_b = project(order_b, (diag_0, diag_1, far_2, side_2, third))
        top_2 = from_peer(far_2[:middle], 1)
        low_2 = from_plane(side_2[middle:], 1)

        side_3, far_3 = gate((side_3, far_3), (top_2, low_2, set_b[2]))
        top_3 = from_peer(far_3[:middle], 1)
        low_3 = from_plane(side_3[middle:], 1)
        order_d = ((1, 6), (0, 7), (1, 5), (1, 7))
        pieces = (far_3, side_3, top_2, low_2, top_3, low_3)

        sources = [*order_a, *order_b, *order_d]
        at_planes = jnp.array([p for p, _ in sources], jnp.int32)
        at_peers = peers[jnp.array([k for _, k in sources], jnp.int32)]
        (places,) = gate((jnp.stack([at_planes, at_peers], axis=1),), (set_b[2],))
        scaled = scaled_rows(places, own_expert, scales, rows, table)
        early = early_grad([set_a[3], set_b[3]], scaled)
        early = early.reshape(slot_dev, CORES, shard_rows, feature_count)
        scaled = scaled.reshape(slot_dev, CORES, shard_rows, -1)
        (given,) = last_grad(1 - core_at, pieces, scaled, early)
        given = from_sibling(given)
        set_d = project(order_d, pieces, keep=False)
        state = last_grad(
            core_at, pieces, scaled, early, (given, master, first_moment, second_moment)
        )

        sets = (set_a, set_b, set_d)
        far_backs = gate([from_plane(s[1], 1) for s in sets], (state[1],))
        hidden_grad = hidden_parts(
            peers,
            plane_at,
            [s[0] for s in sets],
            far_backs,
            [k for p, k in sources if p == 0],
            [k for p, k in sources if p == 1],
        )
        sums = jnp.concatenate([s[2] for s in sets], axis=1)
        ranks = [[sources.index((p, k)) for k in range(dev_count)] for p in range(planes)]
        sums = sums[:, jnp.array(ranks, jnp.int32)[:, position]].transpose(1, 2, 0, 3)
        sums = jnp.stack(by_plane([sums[0], sums[1]])).reshape(-1, slot_dev, tok_rows)
        cores = [
            [(x * CORES + c) * dev_count + d for x in range(planes) for d in range(dev_count)]
            for c in range(CORES)
        ]
        sums = lax.all_to_all(
            sums, ("dp", "expert"), 0, 0, axis_index_groups=cores, tiled=True
        )
        sums = add_planes(sums, state[1]).transpose(0, 2, 1)
        return finish(hidden_grad, sums, state)

    hidden = saved_hidden[0, 0].reshape(dev_count, slot_dev, capacity, planes, plane_rows)

    def hidden_for(shift):
        at = (plane + shift) % planes
        return lax.dynamic_index_in_dim(hidden, at, 3, keepdims=False)

    rows = [hidden_for(0)] + [from_plane(hidden_for(i), i) for i in range(1, planes)]

    own_weight = master.astype(bf16)
    other_weight = from_sibling(own_weight)
    weight = jnp.stack([own_weight, other_weight], axis=1)
    weight = jnp.where(core == 0, weight, weight[:, ::-1]).reshape(width, feature_count)
    before = (jnp.arange(tok_rows)[:, None] > jnp.arange(tok_rows)[None, :]).astype(bf16)
    places = jnp.arange(capacity, dtype=jnp.int32)
    gates = matmul("xqts,sk->xqkt", all_gates, columns)
    live = gates > 0
    spot = matmul("ut,xqkt->xqku", before, live.astype(bf16)).astype(jnp.int32)
    hits = (live[..., None, :] & (spot[..., None, :] == places[:, None])).astype(bf16)
    gates = gates[:, :, : 2 * slot_dev].astype(bf16)

    moved = matmul("xqjat,xqlct->xqjalc", hits[:, :, 2 * slot_dev :], hits[:, :, :slot_dev])
    moved = moved.astype(bf16) * hot_own.T[None, None, :, None, :, None]
    moved = [moved[i] for i in range(planes)]
    hot_rows = [
        matmul("qjalc,qlch->qjah", a, b).astype(bf16) for a, b in zip(moved, by_plane(rows))
    ]
    hot_rows = lax.psum(jnp.stack(hot_rows), "expert")

    def expert_rows(shift, own):
        table = lax.dynamic_index_in_dim(hot_rows, (plane - shift) % planes, 0, keepdims=False)
        picked = own
        for j in range(HOT):
            picked = jnp.where((own_expert == j)[None, :, None, None], table[:, j, None], picked)
        return picked

    def project(tokens, source_gates, source_hits, own):
        count = source_hits.shape[0]
        projected = matmul("td,hd->th", tokens, weight)
        projected = projected.reshape(count, tok_rows, slot_dev, plane_rows)
        slot_hits = source_hits[:, :slot_dev]
        spread = matmul("qlct,qlch->qtlh", slot_hits, own)
        gate_sums = jnp.sum(spread * projected, axis=3)
        scatter = slot_hits * source_gates[:, :slot_dev, None, :]
        back = matmul("qlct,qtlh->qlch", scatter, projected.astype(bf16)).astype(bf16)
        return gate_sums, back

    def scale(source_gates, source_hits, expert_own):
        count = source_hits.shape[0]
        scatter = source_hits[:, slot_dev : 2 * slot_dev] * source_gates[:, slot_dev:, None, :]
        scaled = matmul("qlct,qlch->qtlh", scatter, expert_own).astype(bf16)
        return scaled.reshape(count * tok_rows, width)

    def step(carry, at):
        tokens, total = carry
        shift, own = at
        gathered = lax.all_gather(tokens, "expert", tiled=True)
        source = (plane - shift) % planes
        source_gates = lax.dynamic_index_in_dim(gates, source, 0, keepdims=False)
        source_hits = lax.dynamic_index_in_dim(hits, source, 0, keepdims=False)
        sums, back = project(gathered, source_gates, source_hits, own)
        scaled = scale(source_gates, source_hits, expert_rows(shift, own))
        total = total + matmul("th,td->hd", scaled, gathered)
        return (from_plane(tokens, 1), total), (sums, back)

    start = (grad_out, jnp.zeros((width, feature_count), f32))
    (_, grads), (sums, backs) = lax.scan(step, start, (jnp.arange(planes), jnp.stack(rows)))

    backs = [backs[0]] + [from_plane(backs[i], -i) for i in range(1, planes)]
    order = (jnp.arange(planes) - plane) % planes
    hidden_grad = jnp.concatenate(list(jnp.take(jnp.stack(backs), order, axis=0)), axis=-1)
    gate_sums = sums[0]
    for i in range(1, planes):
        gate_sums = gate_sums + from_plane(sums[i], -i)

    grads = grads.reshape(slot_dev, CORES, shard_rows, feature_count)
    kept = lax.dynamic_index_in_dim(grads, core, 1, keepdims=False)
    given = lax.dynamic_index_in_dim(grads, 1 - core, 1, keepdims=False)
    grad_total = kept + from_sibling(given.astype(bf16)).astype(f32)
    state = adam(grad_total, master, first_moment, second_moment)
    gate_sums = lax.all_to_all(gate_sums, "expert", split_axis=0, concat_axis=0, tiled=True)
    return finish(hidden_grad, gate_sums, state)


def solution(mesh):
    placed = (
        P(("dp", "expert"), None),
        P(("dp", "expert"), None),
        P(("dp", "expert"), None),
        P(("dp", "expert"), None),
        P(),
        P("dp", "expert", None, None, None, None),
        P("expert", "dp", None),
        P("expert", "dp", None),
        P("expert", "dp", None),
    )
    return jax.shard_map(
        on_device,
        mesh=mesh,
        in_specs=placed,
        out_specs=(
            P("dp", "expert", None, None, None, None),
            P(("dp", "expert"), None),
            P("expert", "dp", None),
            P("expert", "dp", None),
            P("expert", "dp", None),
        ),
        check_vma=False,
    )
```

time: 715 us -> 301 us (0.42)
  waiting for transfers between devices: 572 us -> 97.9 us
  Pallas kernels: 0 us -> 111 us
  matrix products: 39.6 us -> 0 us
  local copies, waits for them, and re-layouts: 47 us -> 19.3 us
  starting transfers between devices: 19.4 us -> 46.4 us
  other arithmetic: 22.8 us -> 11.3 us
    psum x1 -> x0, waiting for transfers between devices: 241 us -> none  [on_device(): lax.psum(grad_table.astype(jnp.bfloat16), 'expert').astype(jnp.float32)]
    all_to_all x3, waiting for transfers between devices: 126 us -> 11.9 us  [the longest x1 11.9 us: on_device(): lax.all_to_all(saved_hidden[0, 0], 'expert', split_axis=0, concat_axis=0,...]
    reduce_scatter x1 -> x0, waiting for transfers between devices: 111 us -> none  [on_device(): lax.psum_scatter(jnp.einsum('qlch,qlcd->hld', hidden, scaled, preferred_e...]
    pallas_call x0 -> x20, Pallas kernels: none -> 111 us  [the longest x3 39.4 us: project_set(): pl.pallas_call(body, grid_spec=pltpu.PrefetchScalarGridSpec(num_scalar_pr...]
    all_gather x1, waiting for transfers between devices: 93.2 us -> 0.02 us  [on_device(): lax.all_gather(table[None], 'expert', axis_index_groups=lines, tiled=True)]
    ppermute x0 -> x27, waiting for transfers between devices: none -> 86 us  [the longest x12 43.3 us: from_plane(): return lax.ppermute(value, 'dp', pairs)]
    dot_general x4 -> x0, matrix products: 39.6 us -> none  [the longest x1 14.1 us: on_device(): jnp.einsum('qlch,qlcd->hld', hidden, scaled, preferred_element_type=jnp.f...]
    ppermute x0 -> x27, starting transfers between devices: none -> 32.5 us  [the longest x9 15.8 us: from_peer(): lax.ppermute(value, 'expert', [(i, i ^ bits) for i in range(dev_count)])]
  transfers between devices with their start and end apart: 6 -> 31, of which waited for: 5 -> 12; matrix products, arithmetic and copies ran while one was open for 3% -> 7% of each run, Pallas kernels for 0% -> 32%
where the time goes in v1:
time: 301 us; the launch traced here: 300 us
  Pallas kernels  111 us (37%)
  waiting for transfers between devices  97.9 us (33%)
  starting transfers between devices  46.4 us (15%)
  local copies, waits for them, and re-layouts  19.3 us (6%)
  between operations  14.5 us (5%)
  other arithmetic  11.3 us (4%)
    ppermute x12, waiting for transfers between devices, from_plane(): return lax.ppermute(value, 'dp', pairs)  43.3 us
    pallas_call x3, Pallas kernels, project_set(): pl.pallas_call(body, grid_spec=pltpu.PrefetchScalarGridSpec(num_scalar_pr...  39.4 us
    pallas_call x2, Pallas kernels, last_grad(): pl.pallas_call(body, grid_spec=pltpu.PrefetchScalarGridSpec(num_scalar_pr...  26.8 us
    ppermute x9, waiting for transfers between devices, from_peer(): lax.ppermute(value, 'expert', [(i, i ^ bits) for i in range(dev_count)])  25.9 us
    pallas_call x1, Pallas kernels, early_grad(): pl.pallas_call(body, grid=(features // tile,), in_specs=[pl.BlockSpec((g....  18.2 us
    ppermute x4, waiting for transfers between devices, along(): return lax.ppermute(value, 'expert', pairs)  16.7 us
    ppermute x9, starting transfers between devices, from_peer(): lax.ppermute(value, 'expert', [(i, i ^ bits) for i in range(dev_count)])  15.8 us
    ppermute x12, starting transfers between devices, from_plane(): return lax.ppermute(value, 'dp', pairs)  12.4 us
  transfers between devices with their start and end apart: 31, of which 12 were waited for; matrix products, arithmetic and copies ran while one was open for 7% of the time, Pallas kernels for 32%

profile of v1, /device:TPU:0, one launch (start us, length us, event | category | flops | bytes accessed | tf_op | source)
XLA Modules:
  0.0 300.1 jit_solution(3471151946119861269)
XLA Ops:
  7.2 7.4 %all-to-all-start = ((bf16[8,2,48,1024]{3,2,1,0:T(8,128)(2,1)}), bf16[8,2,48,1024]{3,2,1,0:T(8,128)(2,1)S(1)}, u32[]{:S(2)}, u32[]{:S(2)}) async-start(bf16[8,2,48,1024]{3,2,1,0:T(8,128)(2,1)} %bitcast.43), calls=%async_computation | async-start | bytes 3145728 | tf_op jit(solution)/shard_map/all_to_all | solution.py:560
  16.1 2.0 collective-permute-start.2
  18.9 4.2 %collective-permute-start = (bf16[128,3584]{1,0:T(8,128)(2,1)}, bf16[128,3584]{1,0:T(8,128)(2,1)}, u32[]{:S(2)}, u32[]{:S(2)}) collective-permute-start(bf16[128,3584]{1,0:T(8,128)(2,1)} %refs_0_.3), channel_id=1, source_target_pairs={{0,2},{1,3},{2,0},{3,1},{4,6},{5,7},{6,4},{7,5},{8,10},{9,11},{10,... | collective-permute-start | bytes 2752520 | tf_op jit(solution)/shard_map/ppermute | solution.py:487
  23.0 2.3 shard_map.155
  26.4 11.8 %collective-permute-done.4.refs_2_ = bf16[128,3584]{1,0:T(8,128)(2,1)} collective-permute-done((bf16[128,3584]{1,0:T(8,128)(2,1)}, bf16[128,3584]{1,0:T(8,128)(2,1)}, u32[]{:S(2)}, u32[]{:S(2)}) %collective-permute-start.4) | collective-permute-done | bytes 917536 | tf_op jit(solution)/shard_map/ppermute | solution.py:481
  38.2 2.0 collective-permute-start.5
  41.2 11.9 %all-to-all-done = bf16[8,2,48,1024]{3,2,1,0:T(8,128)(2,1)S(1)} async-done(((bf16[8,2,48,1024]{3,2,1,0:T(8,128)(2,1)}), bf16[8,2,48,1024]{3,2,1,0:T(8,128)(2,1)S(1)}, u32[]{:S(2)}, u32[]{:S(2)}) %all-to-all-start) | async-done | bytes 1572896 | tf_op jit(solution)/shard_map/all_to_all | solution.py:560
  53.8 2.6 all-to-all-start.1
  56.5 6.0 %collective-permute-done.refs_0_ = bf16[128,3584]{1,0:T(8,128)(2,1)} collective-permute-done((bf16[128,3584]{1,0:T(8,128)(2,1)}, bf16[128,3584]{1,0:T(8,128)(2,1)}, u32[]{:S(2)}, u32[]{:S(2)}) %collective-permute-start) | collective-permute-done | bytes 917536 | tf_op jit(solution)/shard_map/ppermute | solution.py:487
  62.4 11.9 %collective-permute-done.5.refs_5_.refs_0_ = bf16[128,3584]{1,0:T(8,128)(2,1)} collective-permute-done((bf16[128,3584]{1,0:T(8,128)(2,1)}, bf16[128,3584]{1,0:T(8,128)(2,1)}, u32[]{:S(2)}, u32[]{:S(2)}) %collective-permute-start.5) | collective-permute-done | bytes 917536 | tf_op jit(solution)/shard_map/ppermute | solution.py:487
  80.4 3.1 %shard_map.157 = bf16[2,3,48,512]{3,2,1,0:T(8,128)(2,1)} custom-call(bf16[32,16]{1,0:T(8,128)(2,1)} %pad_convert_fusion.columns_ref, bf16[128,16]{1,0:T(8,128)(2,1)} %copy.71.refs_6_.gates_ref, bf16[16,48,1024]{2,1,0:T(8,128)(2,1)} %get-tuple-element.45.rows_ref, f32[144,768]{1,0:T(8,128)} %copy.73.pairs_ref), custom_call_target="tpu_custom_call" | custom-call | flops 1 | bytes 1 | tf_op jit(solution)/shard_map/pallas_call | solution.py:191
  87.3 4.8 %shard_map.158 = (bf16[2,8,2,48,128]{4,3,2,1,0:T(8,128)(2,1)}, bf16[2,8,2,48,128]{4,3,2,1,0:T(8,128)(2,1)}, bf16[2,8,2,48,128]{4,3,2,1,0:T(8,128)(2,1)}) custom-call(bf16[16,16]{1,0:T(8,128)(2,1)} %fusion.6.columns_ref, bf16[8,128,16]{2,1,0:T(8,128)(2,1)} %bitcast.51, bf16[8,128,16]{2,1,0:T(8,128)(2,1)} %bitcast.50), custom_call_target="tpu_custom_call" | custom-call | flops 1 | bytes 1 | tf_op jit(solution)/shard_map/pallas_call | solution.py:103
  92.1 6.4 %collective-permute-done.10.refs_5_ = bf16[3,48,512]{2,1,0:T(8,128)(2,1)S(1)} collective-permute-done((bf16[3,48,512]{2,1,0:T(8,128)(2,1)S(1)}, bf16[3,48,512]{2,1,0:T(8,128)(2,1)S(1)}, u32[]{:S(2)}, u32[]{:S(2)}) %collective-permute-start.10) | collective-permute-done | bytes 147488 | tf_op jit(solution)/shard_map/ppermute | solution.py:481
  98.5 3.8 %collective-permute-done.6.refs_1_ = bf16[128,3584]{1,0:T(8,128)(2,1)S(1)} collective-permute-done((bf16[128,3584]{1,0:T(8,128)(2,1)}, bf16[128,3584]{1,0:T(8,128)(2,1)S(1)}, u32[]{:S(2)}, u32[]{:S(2)}) %collective-permute-start.6) | collective-permute-done | bytes 917536 | tf_op jit(solution)/shard_map/ppermute | solution.py:548
  103.6 4.6 %shard_map.160.refs_7_.refs_5_.refs_6_ = bf16[2,256,3584]{2,1,0:T(8,128)(2,1)} custom-call(f32[2,256,3584]{2,1,0:T(8,128)} %refs_9_.1, bf16[128,3584]{1,0:T(8,128)(2,1)} %get-tuple-element.48.refs_1_), custom_call_target="tpu_custom_call" | custom-call | flops 1 | bytes 1 | tf_op jit(solution)/shard_map/pallas_call | solution.py:138
  110.6 1.7 collective-permute-start.25
  112.4 7.7 %collective-permute-done.25.refs_0_ = bf16[2,3,48,512]{3,2,1,0:T(8,128)(2,1)S(1)} collective-permute-done((bf16[2,3,48,512]{3,2,1,0:T(8,128)(2,1)}, bf16[2,3,48,512]{3,2,1,0:T(8,128)(2,1)S(1)}, u32[]{:S(2)}, u32[]{:S(2)}) %collective-permute-start.25) | collective-permute-done | bytes 294944 | tf_op jit(solution)/shard_map/ppermute | solution.py:487
  120.1 12.9 %collective-permute-done.13.refs_1_ = bf16[128,3584]{1,0:T(8,128)(2,1)} collective-permute-done((bf16[128,3584]{1,0:T(8,128)(2,1)S(1)}, bf16[128,3584]{1,0:T(8,128)(2,1)}, u32[]{:S(2)}, u32[]{:S(2)}) %collective-permute-start.13) | collective-permute-done | bytes 917536 | tf_op jit(solution)/shard_map/ppermute | solution.py:548
  136.5 1.7 collective-permute-start.14
  140.3 16.3 %shard_map.161 = (bf16[5,2,48,512]{3,2,1,0:T(8,128)(2,1)}, bf16[2,2,48,512]{3,2,1,0:T(8,128)(2,1)}, f32[2,7,128]{2,1,0:T(8,128)}, bf16[896,3584]{1,0:T(8,128)(2,1)}) custom-call(s32[8]{0:T(128)} %fusion.8.peers_ref, s32[1]{0:T(128)} %bitcast.1.core_ref.chunk_ref, bf16[128,3584]{1,0:T(8,128)(2,1)} %refs_0_.3, bf16[128,3584]{1,0:T(8,128)(2,1)} %get-tuple-element.43.refs_1_, ...), custom_call_target="tpu_custom_call" | custom-call | flops 6576668672 | bytes 20185088 | tf_op jit(solution)/shard_map/pallas_call | solution.py:257
  156.6 2.8 collective-permute-done.15.refs_3_
  159.4 18.2 %collective-permute-done.12.refs_4_.refs_1_ = bf16[128,3584]{1,0:T(8,128)(2,1)S(1)} collective-permute-done((bf16[128,3584]{1,0:T(8,128)(2,1)}, bf16[128,3584]{1,0:T(8,128)(2,1)S(1)}, u32[]{:S(2)}, u32[]{:S(2)}) %collective-permute-start.12) | collective-permute-done | bytes 917536 | tf_op jit(solution)/shard_map/ppermute | solution.py:481
  178.6 2.3 broadcast_select_fusion.refs_4_
  188.2 12.9 %shard_map.163 = (bf16[2,2,48,512]{3,2,1,0:T(8,128)(2,1)}, bf16[3,2,48,512]{3,2,1,0:T(8,128)(2,1)}, f32[2,5,128]{2,1,0:T(8,128)}, bf16[640,3584]{1,0:T(8,128)(2,1)}) custom-call(s32[8]{0:T(128)} %fusion.8.peers_ref, s32[1]{0:T(128)} %bitcast.1.core_ref.chunk_ref, bf16[128,3584]{1,0:T(8,128)(2,1)} %collective-permute-done.5.refs_5_.refs_0_, ...), custom_call_target="tpu_custom_call" | custom-call | flops 4697620480 | bytes 16515072 | tf_op jit(solution)/shard_map/pallas_call | solution.py:257
  201.1 6.7 %shard_map.168.refs_2_ = bf16[1024,2048]{1,0:T(8,128)(2,1)} custom-call(s32[16,2]{1,0:T(8,128)} %shard_map.166.places_ref, s32[2]{0:T(128)} %copy-done.33, bf16[2,8,2,48,128]{4,3,2,1,0:T(8,128)(2,1)} %get-tuple-element.46.refs_6_.scale_ref, bf16[8,2,48,512]{3,2,1,0:T(8,128)(2,1)} %get-tuple-element.53.refs_11_.refs_9_.refs_10_.nr_ref, ...), custom_call_target="tpu_custom_call" | custom-call | flops 1 | bytes 1 | tf_op jit(solution)/shard_map/pallas_call | solution.py:345
  207.8 4.1 %collective-permute-done.19.refs_3_ = bf16[64,3584]{1,0:T(8,128)(2,1)S(1)} collective-permute-done((bf16[64,3584]{1,0:T(8,128)(2,1)}, bf16[64,3584]{1,0:T(8,128)(2,1)S(1)}, u32[]{:S(2)}, u32[]{:S(2)}) %collective-permute-start.19) | collective-permute-done | bytes 458784 | tf_op jit(solution)/shard_map/ppermute | solution.py:481
  219.6 18.2 %shard_map.169 = bf16[1024,3584]{1,0:T(8,128)(2,1)} custom-call(bf16[896,3584]{1,0:T(8,128)(2,1)} %get-tuple-element.70.refs_0_, bf16[640,3584]{1,0:T(8,128)(2,1)} %get-tuple-element.71.refs_1_, bf16[1024,2048]{1,0:T(8,128)(2,1)} %shard_map.168.refs_2_), custom_call_target="tpu_custom_call" | custom-call | flops 15032385536 | bytes 22020096 | tf_op jit(solution)/shard_map/pallas_call | solution.py:378
  238.8 7.2 %shard_map.170 = bf16[2,256,3584]{2,1,0:T(8,128)(2,1)} custom-call(s32[1]{0:T(128)S(6)} %sub.12.chunk_ref, bf16[128,3584]{1,0:T(8,128)(2,1)} %get-tuple-element.63.refs_0_, bf16[128,3584]{1,0:T(8,128)(2,1)} %get-tuple-element.64.refs_1_, bf16[64,3584]{1,0:T(8,128)(2,1)} %copy-done.11, bf16[64,3584]{1,0:T(8,128)(2,1)} %copy-done.10, ...), custom_call_target="tpu_custom_call" | custom-call | flops 1 | bytes 1 | tf_op jit(solution)/shard_map/pallas_call | solution.py:423
  248.9 10.1 %shard_map.165 = (bf16[1,2,48,512]{3,2,1,0:T(8,128)(2,1)}, bf16[3,2,48,512]{3,2,1,0:T(8,128)(2,1)}, f32[2,4,128]{2,1,0:T(4,128)}) custom-call(s32[8]{0:T(128)} %fusion.8.peers_ref, s32[1]{0:T(128)} %bitcast.1.core_ref.chunk_ref, bf16[128,3584]{1,0:T(8,128)(2,1)} %get-tuple-element.63.refs_0_, bf16[128,3584]{1,0:T(8,128)(2,1)} %get-tuple-element.64.refs_1_, ...), custom_call_target="tpu_custom_call" | custom-call | flops 3758096384 | bytes 14680064 | tf_op jit(solution)/shard_map/pallas_call | solution.py:257
  261.6 3.9 %all-to-all-start.2 = ((f32[16,2,128]{2,1,0:T(2,128)}), f32[16,2,128]{2,1,0:T(2,128)S(1)}, u32[]{:S(2)}, u32[]{:S(2)}) async-start(f32[16,2,128]{2,1,0:T(2,128)} %bitcast.22), calls=%async_computation.2 | async-start | bytes 32768 | tf_op jit(solution)/shard_map/all_to_all | solution.py:661
  265.5 19.6 %shard_map.171 = (f32[2,256,3584]{2,1,0:T(8,128)}, bf16[2,256,3584]{2,1,0:T(8,128)(2,1)}, bf16[2,256,3584]{2,1,0:T(8,128)(2,1)}) custom-call(s32[1]{0:T(128)} %bitcast.1.core_ref.chunk_ref, bf16[128,3584]{1,0:T(8,128)(2,1)} %get-tuple-element.63.refs_0_, bf16[128,3584]{1,0:T(8,128)(2,1)} %get-tuple-element.64.refs_1_, bf16[64,3584]{1,0:T(8,128)(2,1)} %copy-done.11, ...), custom_call_target="tpu_custom_call" | custom-call | flops 1879048192 | bytes 47710208 | tf_op jit(solution)/shard_map/pallas_call | solution.py:423
  289.9 3.4 %shard_map.173 = bf16[8,2,48,1024]{3,2,1,0:T(8,128)(2,1)} custom-call(s32[8]{0:T(128)} %fusion.8.peers_ref, s32[1]{0:T(128)} %bitcast.plane_ref, bf16[5,2,48,512]{3,2,1,0:T(8,128)(2,1)} %get-tuple-element.54.refs_0_, bf16[2,2,48,512]{3,2,1,0:T(8,128)(2,1)} %get-tuple-element.61.refs_1_, bf16[1,2,48,512]{3,2,1,0:T(8,128)(2,1)} %get-tuple-element.65.refs_2_, ...), custom_call_target="tpu_custom_call" | custom-call | flops 1 | bytes 1 | tf_op jit(solution)/shard_map/pallas_call | solution.py:311
  (183 shorter events, 50.9 us)
Async XLA Ops:
  7.2 45.9 %all-to-all-start = ((bf16[8,2,48,1024]{3,2,1,0:T(8,128)(2,1)}), bf16[8,2,48,1024]{3,2,1,0:T(8,128)(2,1)S(1)}, u32[]{:S(2)}, u32[]{:S(2)}) async-start(bf16[8,2,48,1024]{3,2,1,0:T(8,128)(2,1)} %bitcast.43), calls=%async_computation | async-start | bytes 3145728 | tf_op jit(solution)/shard_map/all_to_all | solution.py:560
  14.6 23.6 %collective-permute-start.4 = (bf16[128,3584]{1,0:T(8,128)(2,1)}, bf16[128,3584]{1,0:T(8,128)(2,1)}, u32[]{:S(2)}, u32[]{:S(2)}) collective-permute-start(bf16[128,3584]{1,0:T(8,128)(2,1)} %refs_0_.3), channel_id=1, source_target_pairs={{0,16},{8,24},{16,0},{24,8},{1,17},{9,25},{17,1},{25,9},{2,18},{10... | collective-permute-start | bytes 2752520 | tf_op jit(solution)/shard_map/ppermute | solution.py:481
  16.1 40.3 %collective-permute-start.2 = (bf16[128,3584]{1,0:T(8,128)(2,1)}, bf16[128,3584]{1,0:T(8,128)(2,1)}, u32[]{:S(2)}, u32[]{:S(2)}) collective-permute-start(bf16[128,3584]{1,0:T(8,128)(2,1)} %refs_0_.3), channel_id=1, source_target_pairs={{0,1},{1,0},{2,3},{3,2},{4,5},{5,4},{6,7},{7,6},{8,9},{9,8},{10,11... | collective-permute-start | bytes 2752520 | tf_op jit(solution)/shard_map/ppermute | solution.py:487
  18.1 38.3 %collective-permute-start.1 = (bf16[128,3584]{1,0:T(8,128)(2,1)}, bf16[128,3584]{1,0:T(8,128)(2,1)S(1)}, u32[]{:S(2)}, u32[]{:S(2)}) collective-permute-start(bf16[128,3584]{1,0:T(8,128)(2,1)} %refs_0_.3), channel_id=1, source_target_pairs={{2,4},{3,5},{4,2},{5,3},{10,12},{11,13},{12,10},{13,11},{18,20},{1... | collective-permute-start | bytes 2752520 | tf_op jit(solution)/shard_map/ppermute | solution.py:548
  18.9 43.6 %collective-permute-start = (bf16[128,3584]{1,0:T(8,128)(2,1)}, bf16[128,3584]{1,0:T(8,128)(2,1)}, u32[]{:S(2)}, u32[]{:S(2)}) collective-permute-start(bf16[128,3584]{1,0:T(8,128)(2,1)} %refs_0_.3), channel_id=1, source_target_pairs={{0,2},{1,3},{2,0},{3,1},{4,6},{5,7},{6,4},{7,5},{8,10},{9,11},{10,... | collective-permute-start | bytes 2752520 | tf_op jit(solution)/shard_map/ppermute | solution.py:487
  25.3 31.1 %collective-permute-start.3 = (bf16[8,2,48,512]{3,2,1,0:T(8,128)(2,1)}, bf16[8,2,48,512]{3,2,1,0:T(8,128)(2,1)S(1)}, u32[]{:S(2)}, u32[]{:S(2)}) collective-permute-start(bf16[8,2,48,512]{3,2,1,0:T(8,128)(2,1)} %get-tuple-element.42), channel_id=1, source_target_pairs={{0,16},{8,24},{16,0},{24,8},{1,17},{9,25},{17,1},{25,9},{2,18},{10... | collective-permute-start | bytes 2359304 | tf_op jit(solution)/shard_map/ppermute | solution.py:481
  38.2 36.1 %collective-permute-start.5 = (bf16[128,3584]{1,0:T(8,128)(2,1)}, bf16[128,3584]{1,0:T(8,128)(2,1)}, u32[]{:S(2)}, u32[]{:S(2)}) collective-permute-start(bf16[128,3584]{1,0:T(8,128)(2,1)} %collective-permute-done.4.refs_2_), channel_id=1, source_target_pairs={{0,1},{1,0},{2,3},{3,2},{4,5},{5,4},{6,7},{7,6},{8,9},{9,8},{10,11... | collective-permute-start | bytes 2752520 | tf_op jit(solution)/shard_map/ppermute | solution.py:487
  53.8 31.8 %all-to-all-start.1 = ((bf16[32,128,16]{1,2,0:T(8,128)(2,1)}), bf16[32,128,16]{1,2,0:T(8,128)(2,1)S(1)}, u32[]{:S(2)}, u32[]{:S(2)}) async-start(bf16[32,128,16]{1,2,0:T(8,128)(2,1)} %broadcast_in_dim.56), calls=%async_computation.1 | async-start | bytes 262144 | tf_op jit(solution)/shard_map/all_to_all | solution.py:499
  56.4 144.8 %all-gather.3.cloned.1.call-start = ((), (), s32[]{:S(2)}) async-start(), calls=%async_computation.3 | async-start | bytes 2949120 | tf_op jit(solution)/shard_map/all_gather | solution.py:609
  74.4 27.9 %collective-permute-start.9 = (bf16[128,3584]{1,0:T(8,128)(2,1)}, bf16[128,3584]{1,0:T(8,128)(2,1)}, u32[]{:S(2)}, u32[]{:S(2)}) collective-permute-start(bf16[128,3584]{1,0:T(8,128)(2,1)} %get-tuple-element.43.refs_1_), channel_id=1, source_target_pairs={{0,16},{8,24},{16,0},{24,8},{1,17},{9,25},{17,1},{25,9},{2,18},{10... | collective-permute-start | bytes 2752520 | tf_op jit(solution)/shard_map/ppermute | solution.py:481
  76.0 26.3 %collective-permute-start.8 = (bf16[128,3584]{1,0:T(8,128)(2,1)}, bf16[128,3584]{1,0:T(8,128)(2,1)}, u32[]{:S(2)}, u32[]{:S(2)}) collective-permute-start(bf16[128,3584]{1,0:T(8,128)(2,1)} %get-tuple-element.43.refs_1_), channel_id=1, source_target_pairs={{0,1},{1,0},{2,3},{3,2},{4,5},{5,4},{6,7},{7,6},{8,9},{9,8},{10,11... | collective-permute-start | bytes 2752520 | tf_op jit(solution)/shard_map/ppermute | solution.py:487
  76.3 26.1 %collective-permute-start.7 = (bf16[128,3584]{1,0:T(8,128)(2,1)}, bf16[128,3584]{1,0:T(8,128)(2,1)S(1)}, u32[]{:S(2)}, u32[]{:S(2)}) collective-permute-start(bf16[128,3584]{1,0:T(8,128)(2,1)} %get-tuple-element.43.refs_1_), channel_id=1, source_target_pairs={{2,4},{3,5},{4,2},{5,3},{10,12},{11,13},{12,10},{13,11},{18,20},{1... | collective-permute-start | bytes 2752520 | tf_op jit(solution)/shard_map/ppermute | solution.py:548
  77.0 25.3 %collective-permute-start.6 = (bf16[128,3584]{1,0:T(8,128)(2,1)}, bf16[128,3584]{1,0:T(8,128)(2,1)S(1)}, u32[]{:S(2)}, u32[]{:S(2)}) collective-permute-start(bf16[128,3584]{1,0:T(8,128)(2,1)} %get-tuple-element.44.refs_0_), channel_id=1, source_target_pairs={{2,0},{3,1},{4,6},{5,7},{10,8},{11,9},{12,14},{13,15},{18,16},{19,... | collective-permute-start | bytes 2752520 | tf_op jit(solution)/shard_map/ppermute | solution.py:548
  84.5 14.0 %collective-permute-start.10 = (bf16[3,48,512]{2,1,0:T(8,128)(2,1)S(1)}, bf16[3,48,512]{2,1,0:T(8,128)(2,1)S(1)}, u32[]{:S(2)}, u32[]{:S(2)}) collective-permute-start(bf16[3,48,512]{2,1,0:T(8,128)(2,1)S(1)} %get-tuple-element.82), channel_id=1, source_target_pairs={{0,16},{8,24},{16,0},{24,8},{1,17},{9,25},{17,1},{25,9},{2,18},{10... | collective-permute-start | bytes 442376 | tf_op jit(solution)/shard_map/ppermute | solution.py:481
  108.2 26.7 %copy-start.9 = (bf16[128,3584]{1,0:T(8,128)(2,1)S(1)}, bf16[128,3584]{1,0:T(8,128)(2,1)}, u32[]{:S(2)}) copy-start(bf16[128,3584]{1,0:T(8,128)(2,1)} %get-tuple-element.47) | copy-start | bytes 2752516
  108.2 32.1 %collective-permute-start.11 = (bf16[2,256,3584]{2,1,0:T(8,128)(2,1)}, bf16[2,256,3584]{2,1,0:T(8,128)(2,1)}, u32[]{:S(2)}, u32[]{:S(2)}) collective-permute-start(bf16[2,256,3584]{2,1,0:T(8,128)(2,1)} %shard_map.160.refs_7_.refs_5_.refs_6_), channel_id=1, source_target_pairs={{0,8},{8,0},{16,24},{24,16},{1,9},{9,1},{17,25},{25,17},{2,10},{10... | collective-permute-start | bytes 11010056 | tf_op jit(solution)/shard_map/ppermute | solution.py:484
  108.2 24.7 %collective-permute-start.13 = (bf16[128,3584]{1,0:T(8,128)(2,1)S(1)}, bf16[128,3584]{1,0:T(8,128)(2,1)}, u32[]{:S(2)}, u32[]{:S(2)}) collective-permute-start(bf16[128,3584]{1,0:T(8,128)(2,1)S(1)} %copy-done.7), channel_id=1, source_target_pairs={{2,0},{3,1},{4,6},{5,7},{10,8},{11,9},{12,14},{13,15},{18,16},{19,... | collective-permute-start | bytes 2752520 | tf_op jit(solution)/shard_map/ppermute | solution.py:548
  110.6 9.5 %collective-permute-start.25 = (bf16[2,3,48,512]{3,2,1,0:T(8,128)(2,1)}, bf16[2,3,48,512]{3,2,1,0:T(8,128)(2,1)S(1)}, u32[]{:S(2)}, u32[]{:S(2)}) collective-permute-start(bf16[2,3,48,512]{3,2,1,0:T(8,128)(2,1)} %pad_maximum_fusion.1), channel_id=1, source_target_pairs={{0,1},{1,0},{2,3},{3,2},{4,5},{5,4},{6,7},{7,6},{8,9},{9,8},{10,11... | collective-permute-start | bytes 884744 | tf_op jit(solution)/shard_map/ppermute | solution.py:487
  136.0 23.5 %collective-permute-start.15 = (bf16[128,3584]{1,0:T(8,128)(2,1)}, bf16[128,3584]{1,0:T(8,128)(2,1)S(1)}, u32[]{:S(2)}, u32[]{:S(2)}) collective-permute-start(bf16[128,3584]{1,0:T(8,128)(2,1)} %broadcast_select_fusion.1.refs_4_), channel_id=1, source_target_pairs={{0,16},{8,24},{16,0},{24,8},{1,17},{9,25},{17,1},{25,9},{2,18},{10... | collective-permute-start | bytes 2752520 | tf_op jit(solution)/shard_map/ppermute | solution.py:481
  136.5 23.0 %collective-permute-start.14 = (bf16[128,3584]{1,0:T(8,128)(2,1)}, bf16[128,3584]{1,0:T(8,128)(2,1)S(1)}, u32[]{:S(2)}, u32[]{:S(2)}) collective-permute-start(bf16[128,3584]{1,0:T(8,128)(2,1)} %broadcast_select_fusion.1.refs_4_), channel_id=1, source_target_pairs={{0,1},{1,0},{2,3},{3,2},{4,5},{5,4},{6,7},{7,6},{8,9},{9,8},{10,11... | collective-permute-start | bytes 2752520 | tf_op jit(solution)/shard_map/ppermute | solution.py:487
  138.2 39.4 %collective-permute-start.12 = (bf16[128,3584]{1,0:T(8,128)(2,1)}, bf16[128,3584]{1,0:T(8,128)(2,1)S(1)}, u32[]{:S(2)}, u32[]{:S(2)}) collective-permute-start(bf16[128,3584]{1,0:T(8,128)(2,1)} %get-tuple-element.49.refs_5_), channel_id=1, source_target_pairs={{0,16},{8,24},{16,0},{24,8},{1,17},{9,25},{17,1},{25,9},{2,18},{10... | collective-permute-start | bytes 2752520 | tf_op jit(solution)/shard_map/ppermute | solution.py:481
  180.9 31.3 %collective-permute-start.17 = (bf16[128,3584]{1,0:T(8,128)(2,1)}, bf16[128,3584]{1,0:T(8,128)(2,1)S(1)}, u32[]{:S(2)}, u32[]{:S(2)}) collective-permute-start(bf16[128,3584]{1,0:T(8,128)(2,1)} %broadcast_select_fusion.refs_4_), channel_id=1, source_target_pairs={{0,16},{8,24},{16,0},{24,8},{1,17},{9,25},{17,1},{25,9},{2,18},{10... | collective-permute-start | bytes 2752520 | tf_op jit(solution)/shard_map/ppermute | solution.py:481
  181.4 30.8 %collective-permute-start.16 = (bf16[128,3584]{1,0:T(8,128)(2,1)}, bf16[128,3584]{1,0:T(8,128)(2,1)S(1)}, u32[]{:S(2)}, u32[]{:S(2)}) collective-permute-start(bf16[128,3584]{1,0:T(8,128)(2,1)} %broadcast_select_fusion.refs_4_), channel_id=1, source_target_pairs={{0,1},{1,0},{2,3},{3,2},{4,5},{5,4},{6,7},{7,6},{8,9},{9,8},{10,11... | collective-permute-start | bytes 2752520 | tf_op jit(solution)/shard_map/ppermute | solution.py:487
  185.7 26.2 %collective-permute-start.19 = (bf16[64,3584]{1,0:T(8,128)(2,1)}, bf16[64,3584]{1,0:T(8,128)(2,1)S(1)}, u32[]{:S(2)}, u32[]{:S(2)}) collective-permute-start(bf16[64,3584]{1,0:T(8,128)(2,1)} %slice.19), channel_id=1, source_target_pairs={{0,16},{8,24},{16,0},{24,8},{1,17},{9,25},{17,1},{25,9},{2,18},{10... | collective-permute-start | bytes 1376264 | tf_op jit(solution)/shard_map/ppermute | solution.py:481
  187.2 25.0 %collective-permute-start.18 = (bf16[64,3584]{1,0:T(8,128)(2,1)S(1)}, bf16[64,3584]{1,0:T(8,128)(2,1)S(1)}, u32[]{:S(2)}, u32[]{:S(2)}) collective-permute-start(bf16[64,3584]{1,0:T(8,128)(2,1)S(1)} %slice.18), channel_id=1, source_target_pairs={{0,1},{1,0},{2,3},{3,2},{4,5},{5,4},{6,7},{7,6},{8,9},{9,8},{10,11... | collective-permute-start | bytes 1376264 | tf_op jit(solution)/shard_map/ppermute | solution.py:487
  216.3 21.5 %collective-permute-start.21 = (bf16[64,3584]{1,0:T(8,128)(2,1)S(1)}, bf16[64,3584]{1,0:T(8,128)(2,1)S(1)}, u32[]{:S(2)}, u32[]{:S(2)}) collective-permute-start(bf16[64,3584]{1,0:T(8,128)(2,1)S(1)} %slice.21), channel_id=1, source_target_pairs={{0,16},{8,24},{16,0},{24,8},{1,17},{9,25},{17,1},{25,9},{2,18},{10... | collective-permute-start | bytes 1376264 | tf_op jit(solution)/shard_map/ppermute | solution.py:481
  217.9 20.0 %collective-permute-start.20 = (bf16[64,3584]{1,0:T(8,128)(2,1)S(1)}, bf16[64,3584]{1,0:T(8,128)(2,1)S(1)}, u32[]{:S(2)}, u32[]{:S(2)}) collective-permute-start(bf16[64,3584]{1,0:T(8,128)(2,1)S(1)} %slice.20), channel_id=1, source_target_pairs={{0,1},{1,0},{2,3},{3,2},{4,5},{5,4},{6,7},{7,6},{8,9},{9,8},{10,11... | collective-permute-start | bytes 1376264 | tf_op jit(solution)/shard_map/ppermute | solution.py:487
  246.0 19.5 %collective-permute-start.26 = (bf16[2,256,3584]{2,1,0:T(8,128)(2,1)}, bf16[2,256,3584]{2,1,0:T(8,128)(2,1)}, u32[]{:S(2)}, u32[]{:S(2)}) collective-permute-start(bf16[2,256,3584]{2,1,0:T(8,128)(2,1)} %shard_map.170), channel_id=1, source_target_pairs={{0,8},{8,0},{16,24},{24,16},{1,9},{9,1},{17,25},{25,17},{2,10},{10... | collective-permute-start | bytes 11010056 | tf_op jit(solution)/shard_map/ppermute | solution.py:484
  246.8 41.5 %collective-permute-start.22 = (bf16[2,2,48,512]{3,2,1,0:T(8,128)(2,1)S(1)}, bf16[2,2,48,512]{3,2,1,0:T(8,128)(2,1)S(1)}, u32[]{:S(2)}, u32[]{:S(2)}) collective-permute-start(bf16[2,2,48,512]{3,2,1,0:T(8,128)(2,1)S(1)} %copy-done.37), channel_id=1, source_target_pairs={{0,16},{8,24},{16,0},{24,8},{1,17},{9,25},{17,1},{25,9},{2,18},{10... | collective-permute-start | bytes 589832 | tf_op jit(solution)/shard_map/ppermute | solution.py:481
  247.4 40.9 %collective-permute-start.23 = (bf16[3,2,48,512]{3,2,1,0:T(8,128)(2,1)S(1)}, bf16[3,2,48,512]{3,2,1,0:T(8,128)(2,1)S(1)}, u32[]{:S(2)}, u32[]{:S(2)}) collective-permute-start(bf16[3,2,48,512]{3,2,1,0:T(8,128)(2,1)S(1)} %copy-done.36), channel_id=1, source_target_pairs={{0,16},{8,24},{16,0},{24,8},{1,17},{9,25},{17,1},{25,9},{2,18},{10... | collective-permute-start | bytes 884744 | tf_op jit(solution)/shard_map/ppermute | solution.py:481
  259.8 28.6 %collective-permute-start.24 = (bf16[3,2,48,512]{3,2,1,0:T(8,128)(2,1)}, bf16[3,2,48,512]{3,2,1,0:T(8,128)(2,1)S(1)}, u32[]{:S(2)}, u32[]{:S(2)}) collective-permute-start(bf16[3,2,48,512]{3,2,1,0:T(8,128)(2,1)} %get-tuple-element.68), channel_id=1, source_target_pairs={{0,16},{8,24},{16,0},{24,8},{1,17},{9,25},{17,1},{25,9},{2,18},{10... | collective-permute-start | bytes 884744 | tf_op jit(solution)/shard_map/ppermute | solution.py:481
  261.6 23.4 %all-to-all-start.2 = ((f32[16,2,128]{2,1,0:T(2,128)}), f32[16,2,128]{2,1,0:T(2,128)S(1)}, u32[]{:S(2)}, u32[]{:S(2)}) async-start(f32[16,2,128]{2,1,0:T(2,128)} %bitcast.22), calls=%async_computation.2 | async-start | bytes 32768 | tf_op jit(solution)/shard_map/all_to_all | solution.py:661
  (37 other events, 330.6 us)
Sparse Core Ops, SparseCore 0:
  135.0 48.6 all-gather.2

commit v2 on v1

--- a/solution.py
+++ b/solution.py
@@ -602,7 +602,7 @@
         table_side = from_peer(table, 1)
         order_a = ((0, 0), (0, 2), (1, 0), (0, 1), (0, 4), (0, 3), (1, 2))
         set_a = project(order_a, (grad_out, pair, far_0, side_0, second, side_1, far_1))
-        (table_side,) = gate((table_side,), (last,))
+        (table_side,) = gate((table_side,), (last, side_2, far_2))
         even = dev_index % 2 == 0
         table = jnp.stack([jnp.where(even, table, table_side), jnp.where(even, table_side, table)])
         lines = [list(range(y, dev_count, 2)) for y in range(2)]

time: 301 us -> 289 us (0.960)
  waiting for transfers between devices: 97.9 us -> 84.2 us
    ppermute x12, waiting for transfers between devices: 43.3 us -> 21.6 us  [from_plane(): return lax.ppermute(value, 'dp', pairs)]
    ppermute x9, waiting for transfers between devices: 25.9 us -> 43.6 us  [from_peer(): lax.ppermute(value, 'expert', [(i, i ^ bits) for i in range(dev_count)])]
    ppermute x4, waiting for transfers between devices: 16.7 us -> 3.83 us  [along(): return lax.ppermute(value, 'expert', pairs)]
    all_gather x1, waiting for transfers between devices: 0.02 us -> 3.32 us  [on_device(): lax.all_gather(table[None], 'expert', axis_index_groups=lines, tiled=True)]
    unnamed x78 -> x76, local copies, waits for them, and re-layouts: 9 us -> 10.9 us
  transfers between devices with their start and end apart: 31 -> 31, of which waited for: 12 -> 10; matrix products, arithmetic and copies ran while one was open for 7% -> 8% of each run, Pallas kernels for 32% -> 33%
where the time goes in v2:
time: 289 us; the launch traced here: 287 us
  Pallas kernels  111 us (38%)
  waiting for transfers between devices  84.2 us (29%)
  starting transfers between devices  44.4 us (15%)
  local copies, waits for them, and re-layouts  22.3 us (8%)
  between operations  14.5 us (5%)
  other arithmetic  11.2 us (4%)
    ppermute x9, waiting for transfers between devices, from_peer(): lax.ppermute(value, 'expert', [(i, i ^ bits) for i in range(dev_count)])  43.6 us
    pallas_call x3, Pallas kernels, project_set(): pl.pallas_call(body, grid_spec=pltpu.PrefetchScalarGridSpec(num_scalar_pr...  39.6 us
    pallas_call x2, Pallas kernels, last_grad(): pl.pallas_call(body, grid_spec=pltpu.PrefetchScalarGridSpec(num_scalar_pr...  26.7 us
    ppermute x12, waiting for transfers between devices, from_plane(): return lax.ppermute(value, 'dp', pairs)  21.6 us
    pallas_call x1, Pallas kernels, early_grad(): pl.pallas_call(body, grid=(features // tile,), in_specs=[pl.BlockSpec((g....  18.2 us
    ppermute x9, starting transfers between devices, from_peer(): lax.ppermute(value, 'expert', [(i, i ^ bits) for i in range(dev_count)])  14.1 us
    ppermute x12, starting transfers between devices, from_plane(): return lax.ppermute(value, 'dp', pairs)  12.7 us
    all_to_all x1, waiting for transfers between devices, on_device(): lax.all_to_all(saved_hidden[0, 0], 'expert', split_axis=0, concat_axis=0,...  11.9 us
  transfers between devices with their start and end apart: 31, of which 10 were waited for; matrix products, arithmetic and copies ran while one was open for 8% of the time, Pallas kernels for 33%

profile of v2, /device:TPU:0, one launch (start us, length us, event | category | flops | bytes accessed | tf_op | source)
XLA Modules:
  0.0 287.4 jit_solution(11884148975831620389)
XLA Ops:
  7.2 7.4 %all-to-all-start = ((bf16[8,2,48,1024]{3,2,1,0:T(8,128)(2,1)}), bf16[8,2,48,1024]{3,2,1,0:T(8,128)(2,1)S(1)}, u32[]{:S(2)}, u32[]{:S(2)}) async-start(bf16[8,2,48,1024]{3,2,1,0:T(8,128)(2,1)} %bitcast.43), calls=%async_computation | async-start | bytes 3145728 | tf_op jit(solution)/shard_map/all_to_all | solution.py:560
  16.1 2.0 collective-permute-start.2
  18.9 4.2 %collective-permute-start = (bf16[128,3584]{1,0:T(8,128)(2,1)}, bf16[128,3584]{1,0:T(8,128)(2,1)}, u32[]{:S(2)}, u32[]{:S(2)}) collective-permute-start(bf16[128,3584]{1,0:T(8,128)(2,1)} %refs_0_.3), channel_id=1, source_target_pairs={{0,2},{1,3},{2,0},{3,1},{4,6},{5,7},{6,4},{7,5},{8,10},{9,11},{10,... | collective-permute-start | bytes 2752520 | tf_op jit(solution)/shard_map/ppermute | solution.py:487
  23.0 2.3 shard_map.155
  26.4 11.8 %collective-permute-done.4.refs_2_ = bf16[128,3584]{1,0:T(8,128)(2,1)} collective-permute-done((bf16[128,3584]{1,0:T(8,128)(2,1)}, bf16[128,3584]{1,0:T(8,128)(2,1)}, u32[]{:S(2)}, u32[]{:S(2)}) %collective-permute-start.4) | collective-permute-done | bytes 917536 | tf_op jit(solution)/shard_map/ppermute | solution.py:481
  38.2 2.0 collective-permute-start.5
  41.2 11.9 %all-to-all-done = bf16[8,2,48,1024]{3,2,1,0:T(8,128)(2,1)S(1)} async-done(((bf16[8,2,48,1024]{3,2,1,0:T(8,128)(2,1)}), bf16[8,2,48,1024]{3,2,1,0:T(8,128)(2,1)S(1)}, u32[]{:S(2)}, u32[]{:S(2)}) %all-to-all-start) | async-done | bytes 1572896 | tf_op jit(solution)/shard_map/all_to_all | solution.py:560
  53.8 2.6 all-to-all-start.1
  56.5 5.9 %collective-permute-done.refs_0_ = bf16[128,3584]{1,0:T(8,128)(2,1)} collective-permute-done((bf16[128,3584]{1,0:T(8,128)(2,1)}, bf16[128,3584]{1,0:T(8,128)(2,1)}, u32[]{:S(2)}, u32[]{:S(2)}) %collective-permute-start) | collective-permute-done | bytes 917536 | tf_op jit(solution)/shard_map/ppermute | solution.py:487
  62.4 11.9 %collective-permute-done.5.refs_5_.refs_0_ = bf16[128,3584]{1,0:T(8,128)(2,1)} collective-permute-done((bf16[128,3584]{1,0:T(8,128)(2,1)}, bf16[128,3584]{1,0:T(8,128)(2,1)}, u32[]{:S(2)}, u32[]{:S(2)}) %collective-permute-start.5) | collective-permute-done | bytes 917536 | tf_op jit(solution)/shard_map/ppermute | solution.py:487
  74.4 1.6 collective-permute-start.9
  80.4 3.1 %shard_map.157 = bf16[2,3,48,512]{3,2,1,0:T(8,128)(2,1)} custom-call(bf16[32,16]{1,0:T(8,128)(2,1)} %pad_convert_fusion.columns_ref, bf16[128,16]{1,0:T(8,128)(2,1)} %copy.71.refs_6_.gates_ref, bf16[16,48,1024]{2,1,0:T(8,128)(2,1)} %get-tuple-element.45.rows_ref, f32[144,768]{1,0:T(8,128)} %copy.73.pairs_ref), custom_call_target="tpu_custom_call" | custom-call | flops 1 | bytes 1 | tf_op jit(solution)/shard_map/pallas_call | solution.py:191
  87.3 4.8 %shard_map.158 = (bf16[2,8,2,48,128]{4,3,2,1,0:T(8,128)(2,1)}, bf16[2,8,2,48,128]{4,3,2,1,0:T(8,128)(2,1)}, bf16[2,8,2,48,128]{4,3,2,1,0:T(8,128)(2,1)}) custom-call(bf16[16,16]{1,0:T(8,128)(2,1)} %fusion.6.columns_ref, bf16[8,128,16]{2,1,0:T(8,128)(2,1)} %bitcast.51, bf16[8,128,16]{2,1,0:T(8,128)(2,1)} %bitcast.50), custom_call_target="tpu_custom_call" | custom-call | flops 1 | bytes 1 | tf_op jit(solution)/shard_map/pallas_call | solution.py:103
  92.1 6.4 %collective-permute-done.10.refs_5_ = bf16[3,48,512]{2,1,0:T(8,128)(2,1)S(1)} collective-permute-done((bf16[3,48,512]{2,1,0:T(8,128)(2,1)S(1)}, bf16[3,48,512]{2,1,0:T(8,128)(2,1)S(1)}, u32[]{:S(2)}, u32[]{:S(2)}) %collective-permute-start.10) | collective-permute-done | bytes 147488 | tf_op jit(solution)/shard_map/ppermute | solution.py:481
  98.5 3.8 %collective-permute-done.6.refs_1_ = bf16[128,3584]{1,0:T(8,128)(2,1)S(1)} collective-permute-done((bf16[128,3584]{1,0:T(8,128)(2,1)}, bf16[128,3584]{1,0:T(8,128)(2,1)S(1)}, u32[]{:S(2)}, u32[]{:S(2)}) %collective-permute-start.6) | collective-permute-done | bytes 917536 | tf_op jit(solution)/shard_map/ppermute | solution.py:548
  103.6 4.7 %shard_map.160.refs_7_.refs_5_.refs_6_ = bf16[2,256,3584]{2,1,0:T(8,128)(2,1)} custom-call(f32[2,256,3584]{2,1,0:T(8,128)} %refs_9_.1, bf16[128,3584]{1,0:T(8,128)(2,1)} %get-tuple-element.48.refs_1_), custom_call_target="tpu_custom_call" | custom-call | flops 1 | bytes 1 | tf_op jit(solution)/shard_map/pallas_call | solution.py:138
  109.9 1.7 collective-permute-start.14
  114.1 24.8 %collective-permute-done.25.refs_0_ = bf16[2,3,48,512]{3,2,1,0:T(8,128)(2,1)S(1)} collective-permute-done((bf16[2,3,48,512]{3,2,1,0:T(8,128)(2,1)}, bf16[2,3,48,512]{3,2,1,0:T(8,128)(2,1)S(1)}, u32[]{:S(2)}, u32[]{:S(2)}) %collective-permute-start.25) | collective-permute-done | bytes 294944 | tf_op jit(solution)/shard_map/ppermute | solution.py:487
  144.9 16.5 %shard_map.161 = (bf16[5,2,48,512]{3,2,1,0:T(8,128)(2,1)}, bf16[2,2,48,512]{3,2,1,0:T(8,128)(2,1)}, f32[2,7,128]{2,1,0:T(8,128)}, bf16[896,3584]{1,0:T(8,128)(2,1)}) custom-call(s32[8]{0:T(128)} %fusion.8.peers_ref, s32[1]{0:T(128)} %bitcast.1.core_ref.chunk_ref, bf16[128,3584]{1,0:T(8,128)(2,1)} %refs_0_.3, bf16[128,3584]{1,0:T(8,128)(2,1)} %get-tuple-element.43.refs_1_, ...), custom_call_target="tpu_custom_call" | custom-call | flops 6576668672 | bytes 20185088 | tf_op jit(solution)/shard_map/pallas_call | solution.py:257
  161.4 3.3 %collective-permute-done.12.refs_4_.refs_1_ = bf16[128,3584]{1,0:T(8,128)(2,1)S(1)} collective-permute-done((bf16[128,3584]{1,0:T(8,128)(2,1)}, bf16[128,3584]{1,0:T(8,128)(2,1)S(1)}, u32[]{:S(2)}, u32[]{:S(2)}) %collective-permute-start.12) | collective-permute-done | bytes 917536 | tf_op jit(solution)/shard_map/ppermute | solution.py:481
  165.7 2.2 broadcast_select_fusion.refs_4_
  169.4 1.7 collective-permute-start.16
  172.8 1.8 slice.19
  176.2 12.9 %shard_map.163 = (bf16[2,2,48,512]{3,2,1,0:T(8,128)(2,1)}, bf16[3,2,48,512]{3,2,1,0:T(8,128)(2,1)}, f32[2,5,128]{2,1,0:T(8,128)}, bf16[640,3584]{1,0:T(8,128)(2,1)}) custom-call(s32[8]{0:T(128)} %fusion.8.peers_ref, s32[1]{0:T(128)} %bitcast.1.core_ref.chunk_ref, bf16[128,3584]{1,0:T(8,128)(2,1)} %collective-permute-done.5.refs_5_.refs_0_, ...), custom_call_target="tpu_custom_call" | custom-call | flops 4697620480 | bytes 16515072 | tf_op jit(solution)/shard_map/pallas_call | solution.py:257
  189.1 3.3 %all-gather.3.cloned.1.call-done.table_ref = bf16[8,2,3,48,512]{4,3,2,1,0:T(8,128)(2,1)} async-done(((bf16[2,2,3,48,512]{4,3,2,1,0:T(8,128)(2,1)}), bf16[8,2,3,48,512]{4,3,2,1,0:T(8,128)(2,1)}) %all-gather.3.cloned.1.call-update) | async-done | bytes 2359312 | tf_op jit(solution)/shard_map/all_gather | solution.py:609
  192.4 6.7 %shard_map.168.refs_2_ = bf16[1024,2048]{1,0:T(8,128)(2,1)} custom-call(s32[16,2]{1,0:T(8,128)} %shard_map.166.places_ref, s32[2]{0:T(128)} %copy-done.32, bf16[2,8,2,48,128]{4,3,2,1,0:T(8,128)(2,1)} %get-tuple-element.46.refs_6_.scale_ref, bf16[8,2,48,512]{3,2,1,0:T(8,128)(2,1)} %get-tuple-element.53.refs_11_.refs_9_.refs_10_.nr_ref, ...), custom_call_target="tpu_custom_call" | custom-call | flops 1 | bytes 1 | tf_op jit(solution)/shard_map/pallas_call | solution.py:345
  206.4 18.2 %shard_map.169 = bf16[1024,3584]{1,0:T(8,128)(2,1)} custom-call(bf16[896,3584]{1,0:T(8,128)(2,1)} %get-tuple-element.70.refs_0_, bf16[640,3584]{1,0:T(8,128)(2,1)} %get-tuple-element.71.refs_1_, bf16[1024,2048]{1,0:T(8,128)(2,1)} %shard_map.168.refs_2_), custom_call_target="tpu_custom_call" | custom-call | flops 15032385536 | bytes 22020096 | tf_op jit(solution)/shard_map/pallas_call | solution.py:378
  225.6 7.2 %shard_map.170 = bf16[2,256,3584]{2,1,0:T(8,128)(2,1)} custom-call(s32[1]{0:T(128)S(6)} %sub.12.chunk_ref, bf16[128,3584]{1,0:T(8,128)(2,1)} %get-tuple-element.63.refs_0_, bf16[128,3584]{1,0:T(8,128)(2,1)} %get-tuple-element.64.refs_1_, bf16[64,3584]{1,0:T(8,128)(2,1)} %copy-done.13, bf16[64,3584]{1,0:T(8,128)(2,1)} %copy-done.12, ...), custom_call_target="tpu_custom_call" | custom-call | flops 1 | bytes 1 | tf_op jit(solution)/shard_map/pallas_call | solution.py:423
  235.7 10.2 %shard_map.165 = (bf16[1,2,48,512]{3,2,1,0:T(8,128)(2,1)}, bf16[3,2,48,512]{3,2,1,0:T(8,128)(2,1)}, f32[2,4,128]{2,1,0:T(4,128)}) custom-call(s32[8]{0:T(128)} %fusion.8.peers_ref, s32[1]{0:T(128)} %bitcast.1.core_ref.chunk_ref, bf16[128,3584]{1,0:T(8,128)(2,1)} %get-tuple-element.63.refs_0_, bf16[128,3584]{1,0:T(8,128)(2,1)} %get-tuple-element.64.refs_1_, ...), custom_call_target="tpu_custom_call" | custom-call | flops 3758096384 | bytes 14680064 | tf_op jit(solution)/shard_map/pallas_call | solution.py:257
  249.4 3.5 %all-to-all-start.2 = ((f32[16,2,128]{2,1,0:T(2,128)}), f32[16,2,128]{2,1,0:T(2,128)S(1)}, u32[]{:S(2)}, u32[]{:S(2)}) async-start(f32[16,2,128]{2,1,0:T(2,128)} %bitcast.22), calls=%async_computation.2 | async-start | bytes 32768 | tf_op jit(solution)/shard_map/all_to_all | solution.py:661
  252.9 19.5 %shard_map.171 = (f32[2,256,3584]{2,1,0:T(8,128)}, bf16[2,256,3584]{2,1,0:T(8,128)(2,1)}, bf16[2,256,3584]{2,1,0:T(8,128)(2,1)}) custom-call(s32[1]{0:T(128)} %bitcast.1.core_ref.chunk_ref, bf16[128,3584]{1,0:T(8,128)(2,1)} %get-tuple-element.63.refs_0_, bf16[128,3584]{1,0:T(8,128)(2,1)} %get-tuple-element.64.refs_1_, bf16[64,3584]{1,0:T(8,128)(2,1)} %copy-done.13, ...), custom_call_target="tpu_custom_call" | custom-call | flops 1879048192 | bytes 47710208 | tf_op jit(solution)/shard_map/pallas_call | solution.py:423
  277.2 3.4 %shard_map.173 = bf16[8,2,48,1024]{3,2,1,0:T(8,128)(2,1)} custom-call(s32[8]{0:T(128)} %fusion.8.peers_ref, s32[1]{0:T(128)} %bitcast.plane_ref, bf16[5,2,48,512]{3,2,1,0:T(8,128)(2,1)} %get-tuple-element.54.refs_0_, bf16[2,2,48,512]{3,2,1,0:T(8,128)(2,1)} %get-tuple-element.61.refs_1_, bf16[1,2,48,512]{3,2,1,0:T(8,128)(2,1)} %get-tuple-element.65.refs_2_, ...), custom_call_target="tpu_custom_call" | custom-call | flops 1 | bytes 1 | tf_op jit(solution)/shard_map/pallas_call | solution.py:311
  (181 shorter events, 49.4 us)
Async XLA Ops:
  7.2 45.9 %all-to-all-start = ((bf16[8,2,48,1024]{3,2,1,0:T(8,128)(2,1)}), bf16[8,2,48,1024]{3,2,1,0:T(8,128)(2,1)S(1)}, u32[]{:S(2)}, u32[]{:S(2)}) async-start(bf16[8,2,48,1024]{3,2,1,0:T(8,128)(2,1)} %bitcast.43), calls=%async_computation | async-start | bytes 3145728 | tf_op jit(solution)/shard_map/all_to_all | solution.py:560
  14.6 23.6 %collective-permute-start.4 = (bf16[128,3584]{1,0:T(8,128)(2,1)}, bf16[128,3584]{1,0:T(8,128)(2,1)}, u32[]{:S(2)}, u32[]{:S(2)}) collective-permute-start(bf16[128,3584]{1,0:T(8,128)(2,1)} %refs_0_.3), channel_id=1, source_target_pairs={{0,16},{8,24},{16,0},{24,8},{1,17},{9,25},{17,1},{25,9},{2,18},{10... | collective-permute-start | bytes 2752520 | tf_op jit(solution)/shard_map/ppermute | solution.py:481
  16.1 40.3 %collective-permute-start.2 = (bf16[128,3584]{1,0:T(8,128)(2,1)}, bf16[128,3584]{1,0:T(8,128)(2,1)}, u32[]{:S(2)}, u32[]{:S(2)}) collective-permute-start(bf16[128,3584]{1,0:T(8,128)(2,1)} %refs_0_.3), channel_id=1, source_target_pairs={{0,1},{1,0},{2,3},{3,2},{4,5},{5,4},{6,7},{7,6},{8,9},{9,8},{10,11... | collective-permute-start | bytes 2752520 | tf_op jit(solution)/shard_map/ppermute | solution.py:487
  18.1 38.3 %collective-permute-start.1 = (bf16[128,3584]{1,0:T(8,128)(2,1)}, bf16[128,3584]{1,0:T(8,128)(2,1)S(1)}, u32[]{:S(2)}, u32[]{:S(2)}) collective-permute-start(bf16[128,3584]{1,0:T(8,128)(2,1)} %refs_0_.3), channel_id=1, source_target_pairs={{2,4},{3,5},{4,2},{5,3},{10,12},{11,13},{12,10},{13,11},{18,20},{1... | collective-permute-start | bytes 2752520 | tf_op jit(solution)/shard_map/ppermute | solution.py:548
  18.9 43.6 %collective-permute-start = (bf16[128,3584]{1,0:T(8,128)(2,1)}, bf16[128,3584]{1,0:T(8,128)(2,1)}, u32[]{:S(2)}, u32[]{:S(2)}) collective-permute-start(bf16[128,3584]{1,0:T(8,128)(2,1)} %refs_0_.3), channel_id=1, source_target_pairs={{0,2},{1,3},{2,0},{3,1},{4,6},{5,7},{6,4},{7,5},{8,10},{9,11},{10,... | collective-permute-start | bytes 2752520 | tf_op jit(solution)/shard_map/ppermute | solution.py:487
  25.3 31.1 %collective-permute-start.3 = (bf16[8,2,48,512]{3,2,1,0:T(8,128)(2,1)}, bf16[8,2,48,512]{3,2,1,0:T(8,128)(2,1)S(1)}, u32[]{:S(2)}, u32[]{:S(2)}) collective-permute-start(bf16[8,2,48,512]{3,2,1,0:T(8,128)(2,1)} %get-tuple-element.42), channel_id=1, source_target_pairs={{0,16},{8,24},{16,0},{24,8},{1,17},{9,25},{17,1},{25,9},{2,18},{10... | collective-permute-start | bytes 2359304 | tf_op jit(solution)/shard_map/ppermute | solution.py:481
  38.2 36.1 %collective-permute-start.5 = (bf16[128,3584]{1,0:T(8,128)(2,1)}, bf16[128,3584]{1,0:T(8,128)(2,1)}, u32[]{:S(2)}, u32[]{:S(2)}) collective-permute-start(bf16[128,3584]{1,0:T(8,128)(2,1)} %collective-permute-done.4.refs_2_), channel_id=1, source_target_pairs={{0,1},{1,0},{2,3},{3,2},{4,5},{5,4},{6,7},{7,6},{8,9},{9,8},{10,11... | collective-permute-start | bytes 2752520 | tf_op jit(solution)/shard_map/ppermute | solution.py:487
  53.8 31.8 %all-to-all-start.1 = ((bf16[32,128,16]{1,2,0:T(8,128)(2,1)}), bf16[32,128,16]{1,2,0:T(8,128)(2,1)S(1)}, u32[]{:S(2)}, u32[]{:S(2)}) async-start(bf16[32,128,16]{1,2,0:T(8,128)(2,1)} %broadcast_in_dim.56), calls=%async_computation.1 | async-start | bytes 262144 | tf_op jit(solution)/shard_map/all_to_all | solution.py:499
  56.4 136.1 %all-gather.3.cloned.1.call-start = ((), (), s32[]{:S(2)}) async-start(), calls=%async_computation.3 | async-start | bytes 2949120 | tf_op jit(solution)/shard_map/all_gather | solution.py:609
  74.4 27.9 %collective-permute-start.9 = (bf16[128,3584]{1,0:T(8,128)(2,1)}, bf16[128,3584]{1,0:T(8,128)(2,1)}, u32[]{:S(2)}, u32[]{:S(2)}) collective-permute-start(bf16[128,3584]{1,0:T(8,128)(2,1)} %get-tuple-element.43.refs_1_), channel_id=1, source_target_pairs={{0,16},{8,24},{16,0},{24,8},{1,17},{9,25},{17,1},{25,9},{2,18},{10... | collective-permute-start | bytes 2752520 | tf_op jit(solution)/shard_map/ppermute | solution.py:481
  76.0 26.3 %collective-permute-start.8 = (bf16[128,3584]{1,0:T(8,128)(2,1)}, bf16[128,3584]{1,0:T(8,128)(2,1)}, u32[]{:S(2)}, u32[]{:S(2)}) collective-permute-start(bf16[128,3584]{1,0:T(8,128)(2,1)} %get-tuple-element.43.refs_1_), channel_id=1, source_target_pairs={{0,1},{1,0},{2,3},{3,2},{4,5},{5,4},{6,7},{7,6},{8,9},{9,8},{10,11... | collective-permute-start | bytes 2752520 | tf_op jit(solution)/shard_map/ppermute | solution.py:487
  76.3 26.1 %collective-permute-start.7 = (bf16[128,3584]{1,0:T(8,128)(2,1)}, bf16[128,3584]{1,0:T(8,128)(2,1)S(1)}, u32[]{:S(2)}, u32[]{:S(2)}) collective-permute-start(bf16[128,3584]{1,0:T(8,128)(2,1)} %get-tuple-element.43.refs_1_), channel_id=1, source_target_pairs={{2,4},{3,5},{4,2},{5,3},{10,12},{11,13},{12,10},{13,11},{18,20},{1... | collective-permute-start | bytes 2752520 | tf_op jit(solution)/shard_map/ppermute | solution.py:548
  77.0 25.3 %collective-permute-start.6 = (bf16[128,3584]{1,0:T(8,128)(2,1)}, bf16[128,3584]{1,0:T(8,128)(2,1)S(1)}, u32[]{:S(2)}, u32[]{:S(2)}) collective-permute-start(bf16[128,3584]{1,0:T(8,128)(2,1)} %get-tuple-element.44.refs_0_), channel_id=1, source_target_pairs={{2,0},{3,1},{4,6},{5,7},{10,8},{11,9},{12,14},{13,15},{18,16},{19,... | collective-permute-start | bytes 2752520 | tf_op jit(solution)/shard_map/ppermute | solution.py:548
  79.0 24.6 %copy-start.32 = (s32[2]{0:T(128)}, s32[2]{0:T(128)S(1)}, u32[]{:S(2)}) copy-start(s32[2]{0:T(128)S(1)} %dynamic_slice.20.expert_ref) | copy-start | bytes 28
  84.5 14.0 %collective-permute-start.10 = (bf16[3,48,512]{2,1,0:T(8,128)(2,1)S(1)}, bf16[3,48,512]{2,1,0:T(8,128)(2,1)S(1)}, u32[]{:S(2)}, u32[]{:S(2)}) collective-permute-start(bf16[3,48,512]{2,1,0:T(8,128)(2,1)S(1)} %get-tuple-element.82), channel_id=1, source_target_pairs={{0,16},{8,24},{16,0},{24,8},{1,17},{9,25},{17,1},{25,9},{2,18},{10... | collective-permute-start | bytes 442376 | tf_op jit(solution)/shard_map/ppermute | solution.py:481
  108.3 36.6 %collective-permute-start.11 = (bf16[2,256,3584]{2,1,0:T(8,128)(2,1)}, bf16[2,256,3584]{2,1,0:T(8,128)(2,1)}, u32[]{:S(2)}, u32[]{:S(2)}) collective-permute-start(bf16[2,256,3584]{2,1,0:T(8,128)(2,1)} %shard_map.160.refs_7_.refs_5_.refs_6_), channel_id=1, source_target_pairs={{0,8},{8,0},{16,24},{24,16},{1,9},{9,1},{17,25},{25,17},{2,10},{10... | collective-permute-start | bytes 11010056 | tf_op jit(solution)/shard_map/ppermute | solution.py:484
  109.3 29.6 %collective-permute-start.15 = (bf16[128,3584]{1,0:T(8,128)(2,1)}, bf16[128,3584]{1,0:T(8,128)(2,1)S(1)}, u32[]{:S(2)}, u32[]{:S(2)}) collective-permute-start(bf16[128,3584]{1,0:T(8,128)(2,1)} %broadcast_select_fusion.1.refs_4_), channel_id=1, source_target_pairs={{0,16},{8,24},{16,0},{24,8},{1,17},{9,25},{17,1},{25,9},{2,18},{10... | collective-permute-start | bytes 2752520 | tf_op jit(solution)/shard_map/ppermute | solution.py:481
  109.9 29.1 %collective-permute-start.14 = (bf16[128,3584]{1,0:T(8,128)(2,1)}, bf16[128,3584]{1,0:T(8,128)(2,1)}, u32[]{:S(2)}, u32[]{:S(2)}) collective-permute-start(bf16[128,3584]{1,0:T(8,128)(2,1)} %broadcast_select_fusion.1.refs_4_), channel_id=1, source_target_pairs={{0,1},{1,0},{2,3},{3,2},{4,5},{5,4},{6,7},{7,6},{8,9},{9,8},{10,11... | collective-permute-start | bytes 2752520 | tf_op jit(solution)/shard_map/ppermute | solution.py:487
  111.6 27.3 %collective-permute-start.13 = (bf16[128,3584]{1,0:T(8,128)(2,1)S(1)}, bf16[128,3584]{1,0:T(8,128)(2,1)S(1)}, u32[]{:S(2)}, u32[]{:S(2)}) collective-permute-start(bf16[128,3584]{1,0:T(8,128)(2,1)S(1)} %copy-done.7), channel_id=1, source_target_pairs={{2,0},{3,1},{4,6},{5,7},{10,8},{11,9},{12,14},{13,15},{18,16},{19,... | collective-permute-start | bytes 2752520 | tf_op jit(solution)/shard_map/ppermute | solution.py:548
  113.8 25.1 %collective-permute-start.25 = (bf16[2,3,48,512]{3,2,1,0:T(8,128)(2,1)}, bf16[2,3,48,512]{3,2,1,0:T(8,128)(2,1)S(1)}, u32[]{:S(2)}, u32[]{:S(2)}) collective-permute-start(bf16[2,3,48,512]{3,2,1,0:T(8,128)(2,1)} %pad_maximum_fusion.1), channel_id=1, source_target_pairs={{0,1},{1,0},{2,3},{3,2},{4,5},{5,4},{6,7},{7,6},{8,9},{9,8},{10,11... | collective-permute-start | bytes 884744 | tf_op jit(solution)/shard_map/ppermute | solution.py:487
  142.8 22.0 %collective-permute-start.12 = (bf16[128,3584]{1,0:T(8,128)(2,1)}, bf16[128,3584]{1,0:T(8,128)(2,1)S(1)}, u32[]{:S(2)}, u32[]{:S(2)}) collective-permute-start(bf16[128,3584]{1,0:T(8,128)(2,1)} %get-tuple-element.49.refs_5_), channel_id=1, source_target_pairs={{0,16},{8,24},{16,0},{24,8},{1,17},{9,25},{17,1},{25,9},{2,18},{10... | collective-permute-start | bytes 2752520 | tf_op jit(solution)/shard_map/ppermute | solution.py:481
  167.9 32.1 %collective-permute-start.17 = (bf16[128,3584]{1,0:T(8,128)(2,1)}, bf16[128,3584]{1,0:T(8,128)(2,1)S(1)}, u32[]{:S(2)}, u32[]{:S(2)}) collective-permute-start(bf16[128,3584]{1,0:T(8,128)(2,1)} %broadcast_select_fusion.refs_4_), channel_id=1, source_target_pairs={{0,16},{8,24},{16,0},{24,8},{1,17},{9,25},{17,1},{25,9},{2,18},{10... | collective-permute-start | bytes 2752520 | tf_op jit(solution)/shard_map/ppermute | solution.py:481
  169.4 30.7 %collective-permute-start.16 = (bf16[128,3584]{1,0:T(8,128)(2,1)}, bf16[128,3584]{1,0:T(8,128)(2,1)S(1)}, u32[]{:S(2)}, u32[]{:S(2)}) collective-permute-start(bf16[128,3584]{1,0:T(8,128)(2,1)} %broadcast_select_fusion.refs_4_), channel_id=1, source_target_pairs={{0,1},{1,0},{2,3},{3,2},{4,5},{5,4},{6,7},{7,6},{8,9},{9,8},{10,11... | collective-permute-start | bytes 2752520 | tf_op jit(solution)/shard_map/ppermute | solution.py:487
  174.6 24.5 %collective-permute-start.19 = (bf16[64,3584]{1,0:T(8,128)(2,1)}, bf16[64,3584]{1,0:T(8,128)(2,1)S(1)}, u32[]{:S(2)}, u32[]{:S(2)}) collective-permute-start(bf16[64,3584]{1,0:T(8,128)(2,1)} %slice.19), channel_id=1, source_target_pairs={{0,16},{8,24},{16,0},{24,8},{1,17},{9,25},{17,1},{25,9},{2,18},{10... | collective-permute-start | bytes 1376264 | tf_op jit(solution)/shard_map/ppermute | solution.py:481
  175.2 24.9 %collective-permute-start.18 = (bf16[64,3584]{1,0:T(8,128)(2,1)S(1)}, bf16[64,3584]{1,0:T(8,128)(2,1)S(1)}, u32[]{:S(2)}, u32[]{:S(2)}) collective-permute-start(bf16[64,3584]{1,0:T(8,128)(2,1)S(1)} %slice.18), channel_id=1, source_target_pairs={{0,1},{1,0},{2,3},{3,2},{4,5},{5,4},{6,7},{7,6},{8,9},{9,8},{10,11... | collective-permute-start | bytes 1376264 | tf_op jit(solution)/shard_map/ppermute | solution.py:487
  204.2 20.5 %collective-permute-start.21 = (bf16[64,3584]{1,0:T(8,128)(2,1)S(1)}, bf16[64,3584]{1,0:T(8,128)(2,1)S(1)}, u32[]{:S(2)}, u32[]{:S(2)}) collective-permute-start(bf16[64,3584]{1,0:T(8,128)(2,1)S(1)} %slice.21), channel_id=1, source_target_pairs={{0,16},{8,24},{16,0},{24,8},{1,17},{9,25},{17,1},{25,9},{2,18},{10... | collective-permute-start | bytes 1376264 | tf_op jit(solution)/shard_map/ppermute | solution.py:481
  204.9 19.7 %collective-permute-start.20 = (bf16[64,3584]{1,0:T(8,128)(2,1)S(1)}, bf16[64,3584]{1,0:T(8,128)(2,1)S(1)}, u32[]{:S(2)}, u32[]{:S(2)}) collective-permute-start(bf16[64,3584]{1,0:T(8,128)(2,1)S(1)} %slice.20), channel_id=1, source_target_pairs={{0,1},{1,0},{2,3},{3,2},{4,5},{5,4},{6,7},{7,6},{8,9},{9,8},{10,11... | collective-permute-start | bytes 1376264 | tf_op jit(solution)/shard_map/ppermute | solution.py:487
  232.8 20.1 %collective-permute-start.26 = (bf16[2,256,3584]{2,1,0:T(8,128)(2,1)}, bf16[2,256,3584]{2,1,0:T(8,128)(2,1)}, u32[]{:S(2)}, u32[]{:S(2)}) collective-permute-start(bf16[2,256,3584]{2,1,0:T(8,128)(2,1)} %shard_map.170), channel_id=1, source_target_pairs={{0,8},{8,0},{16,24},{24,16},{1,9},{9,1},{17,25},{25,17},{2,10},{10... | collective-permute-start | bytes 11010056 | tf_op jit(solution)/shard_map/ppermute | solution.py:484
  233.6 42.1 %collective-permute-start.22 = (bf16[2,2,48,512]{3,2,1,0:T(8,128)(2,1)S(1)}, bf16[2,2,48,512]{3,2,1,0:T(8,128)(2,1)S(1)}, u32[]{:S(2)}, u32[]{:S(2)}) collective-permute-start(bf16[2,2,48,512]{3,2,1,0:T(8,128)(2,1)S(1)} %copy-done.36), channel_id=1, source_target_pairs={{0,16},{8,24},{16,0},{24,8},{1,17},{9,25},{17,1},{25,9},{2,18},{10... | collective-permute-start | bytes 589832 | tf_op jit(solution)/shard_map/ppermute | solution.py:481
  235.2 40.6 %collective-permute-start.23 = (bf16[3,2,48,512]{3,2,1,0:T(8,128)(2,1)S(1)}, bf16[3,2,48,512]{3,2,1,0:T(8,128)(2,1)S(1)}, u32[]{:S(2)}, u32[]{:S(2)}) collective-permute-start(bf16[3,2,48,512]{3,2,1,0:T(8,128)(2,1)S(1)} %copy-done.35), channel_id=1, source_target_pairs={{0,16},{8,24},{16,0},{24,8},{1,17},{9,25},{17,1},{25,9},{2,18},{10... | collective-permute-start | bytes 884744 | tf_op jit(solution)/shard_map/ppermute | solution.py:481
  246.6 29.1 %collective-permute-start.24 = (bf16[3,2,48,512]{3,2,1,0:T(8,128)(2,1)}, bf16[3,2,48,512]{3,2,1,0:T(8,128)(2,1)S(1)}, u32[]{:S(2)}, u32[]{:S(2)}) collective-permute-start(bf16[3,2,48,512]{3,2,1,0:T(8,128)(2,1)} %get-tuple-element.68), channel_id=1, source_target_pairs={{0,16},{8,24},{16,0},{24,8},{1,17},{9,25},{17,1},{25,9},{2,18},{10... | collective-permute-start | bytes 884744 | tf_op jit(solution)/shard_map/ppermute | solution.py:481
  249.4 23.1 %all-to-all-start.2 = ((f32[16,2,128]{2,1,0:T(2,128)}), f32[16,2,128]{2,1,0:T(2,128)S(1)}, u32[]{:S(2)}, u32[]{:S(2)}) async-start(f32[16,2,128]{2,1,0:T(2,128)} %bitcast.22), calls=%async_computation.2 | async-start | bytes 32768 | tf_op jit(solution)/shard_map/all_to_all | solution.py:661
  (36 other events, 244.1 us)
Sparse Core Ops, SparseCore 0:
  142.9 49.5 all-gather.2

commit v3 on v2

--- a/solution.py
+++ b/solution.py
@@ -292,7 +292,7 @@
     )(peers, core, *pieces, *weights, hits, backs, *rows)
 
 
-def hidden_parts(peers, plane, near, far, near_order, far_order):
+def hidden_parts(peers, plane, near, far, wait, near_order, far_order):
     slot_dev, capacity, plane_rows = near[0].shape[1:]
     devs = peers.shape[0]
 
@@ -300,7 +300,7 @@
         out_ref = refs[-1]
         for arrays, order, flip in (
             (refs[: len(near)], near_order, 0),
-            (refs[len(near) : -1], far_order, 1),
+            (refs[len(near) : -2], far_order, 1),
         ):
             half = pl.multiple_of((plane_ref[0] ^ flip) * plane_rows, plane_rows)
             flat = [ref.at[i] for ref in arrays for i in range(ref.shape[0])]
@@ -313,13 +313,14 @@
         grid_spec=pltpu.PrefetchScalarGridSpec(
             num_scalar_prefetch=2,
             grid=(1,),
-            in_specs=[whole_spec(v.shape) for v in (*near, *far)],
+            in_specs=[whole_spec(v.shape) for v in (*near, *far)]
+            + [pl.BlockSpec(memory_space=pl.ANY)],
             out_specs=whole_spec(shape),
         ),
         out_shape=jax.ShapeDtypeStruct(shape, bf16),
         compiler_params=kernel_params(),
         cost_estimate=light(),
-    )(peers, plane, *near, *far)
+    )(peers, plane, *near, *far, wait)
 
 
 def scaled_rows(places, own_expert, scales, rows, table):
@@ -598,11 +599,10 @@
         last = along(moved_pair, outward)
         side_2, far_2 = from_peer(second, 1), from_plane(second, 1)
         diag_1 = from_plane(side_1, 1)
-        table = jnp.stack([table[0], table_far])
+        (table,) = gate((jnp.stack([table[0], table_far]),), (last, side_2, far_2))
         table_side = from_peer(table, 1)
         order_a = ((0, 0), (0, 2), (1, 0), (0, 1), (0, 4), (0, 3), (1, 2))
         set_a = project(order_a, (grad_out, pair, far_0, side_0, second, side_1, far_1))
-        (table_side,) = gate((table_side,), (last, side_2, far_2))
         even = dev_index % 2 == 0
         table = jnp.stack([jnp.where(even, table, table_side), jnp.where(even, table_side, table)])
         lines = [list(range(y, dev_count, 2)) for y in range(2)]
@@ -641,12 +641,13 @@
         )
 
         sets = (set_a, set_b, set_d)
-        far_backs = gate([from_plane(s[1], 1) for s in sets], (state[1],))
+        far_backs = [from_plane(s[1], 1) for s in sets]
         hidden_grad = hidden_parts(
             peers,
             plane_at,
             [s[0] for s in sets],
             far_backs,
+            state[1],
             [k for p, k in sources if p == 0],
             [k for p, k in sources if p == 1],
         )

time: 289 us -> 295 us (1.021)
  waiting for transfers between devices: 84.2 us -> 90.4 us
    ppermute x12, waiting for transfers between devices: 21.6 us -> 44.8 us  [from_plane(): return lax.ppermute(value, 'dp', pairs)]
    ppermute x9, waiting for transfers between devices: 43.6 us -> 26.7 us  [from_peer(): lax.ppermute(value, 'expert', [(i, i ^ bits) for i in range(dev_count)])]
    all_gather x1, waiting for transfers between devices: 3.32 us -> 0.01 us  [on_device(): lax.all_gather(table[None], 'expert', axis_index_groups=lines, tiled=True)]
    ppermute x4, waiting for transfers between devices: 3.83 us -> 7.07 us  [along(): return lax.ppermute(value, 'expert', pairs)]
    unnamed x76 -> x94, local copies, waits for them, and re-layouts: 10.9 us -> 9.66 us
  transfers between devices with their start and end apart: 31 -> 31, of which waited for: 10 -> 13; matrix products, arithmetic and copies ran while one was open for 8% -> 9% of each run, Pallas kernels for 33% -> 33%
where the time goes in v3:
time: 295 us; the launch traced here: 293 us
  Pallas kernels  111 us (38%)
  waiting for transfers between devices  90.4 us (31%)
  starting transfers between devices  44 us (15%)
  local copies, waits for them, and re-layouts  22.5 us (8%)
  between operations  14.6 us (5%)
  other arithmetic  10.9 us (4%)
    ppermute x12, waiting for transfers between devices, from_plane(): return lax.ppermute(value, 'dp', pairs)  44.8 us
    pallas_call x3, Pallas kernels, project_set(): pl.pallas_call(body, grid_spec=pltpu.PrefetchScalarGridSpec(num_scalar_pr...  39.8 us
    pallas_call x2, Pallas kernels, last_grad(): pl.pallas_call(body, grid_spec=pltpu.PrefetchScalarGridSpec(num_scalar_pr...  26.7 us
    ppermute x9, waiting for transfers between devices, from_peer(): lax.ppermute(value, 'expert', [(i, i ^ bits) for i in range(dev_count)])  26.7 us
    pallas_call x1, Pallas kernels, early_grad(): pl.pallas_call(body, grid=(features // tile,), in_specs=[pl.BlockSpec((g....  18.2 us
    ppermute x9, starting transfers between devices, from_peer(): lax.ppermute(value, 'expert', [(i, i ^ bits) for i in range(dev_count)])  12.9 us
    ppermute x12, starting transfers between devices, from_plane(): return lax.ppermute(value, 'dp', pairs)  12.5 us
    all_to_all x1, waiting for transfers between devices, on_device(): lax.all_to_all(saved_hidden[0, 0], 'expert', split_axis=0, concat_axis=0,...  11.9 us
  transfers between devices with their start and end apart: 31, of which 13 were waited for; matrix products, arithmetic and copies ran while one was open for 9% of the time, Pallas kernels for 33%

profile of v3, /device:TPU:0, one launch (start us, length us, event | category | flops | bytes accessed | tf_op | source)
XLA Modules:
  0.0 293.4 jit_solution(13319783902619262400)
XLA Ops:
  7.2 7.4 %all-to-all-start = ((bf16[8,2,48,1024]{3,2,1,0:T(8,128)(2,1)}), bf16[8,2,48,1024]{3,2,1,0:T(8,128)(2,1)S(1)}, u32[]{:S(2)}, u32[]{:S(2)}) async-start(bf16[8,2,48,1024]{3,2,1,0:T(8,128)(2,1)} %bitcast.43), calls=%async_computation | async-start | bytes 3145728 | tf_op jit(solution)/shard_map/all_to_all | solution.py:561
  16.1 2.0 collective-permute-start.2
  18.9 4.2 %collective-permute-start = (bf16[128,3584]{1,0:T(8,128)(2,1)}, bf16[128,3584]{1,0:T(8,128)(2,1)}, u32[]{:S(2)}, u32[]{:S(2)}) collective-permute-start(bf16[128,3584]{1,0:T(8,128)(2,1)} %refs_0_.3), channel_id=1, source_target_pairs={{0,2},{1,3},{2,0},{3,1},{4,6},{5,7},{6,4},{7,5},{8,10},{9,11},{10,... | collective-permute-start | bytes 2752520 | tf_op jit(solution)/shard_map/ppermute | solution.py:488
  23.0 2.3 shard_map.155
  26.4 11.8 %collective-permute-done.4.refs_2_ = bf16[128,3584]{1,0:T(8,128)(2,1)} collective-permute-done((bf16[128,3584]{1,0:T(8,128)(2,1)}, bf16[128,3584]{1,0:T(8,128)(2,1)}, u32[]{:S(2)}, u32[]{:S(2)}) %collective-permute-start.4) | collective-permute-done | bytes 917536 | tf_op jit(solution)/shard_map/ppermute | solution.py:482
  38.2 2.0 collective-permute-start.5
  41.2 11.9 %all-to-all-done = bf16[8,2,48,1024]{3,2,1,0:T(8,128)(2,1)S(1)} async-done(((bf16[8,2,48,1024]{3,2,1,0:T(8,128)(2,1)}), bf16[8,2,48,1024]{3,2,1,0:T(8,128)(2,1)S(1)}, u32[]{:S(2)}, u32[]{:S(2)}) %all-to-all-start) | async-done | bytes 1572896 | tf_op jit(solution)/shard_map/all_to_all | solution.py:561
  53.8 3.3 %all-to-all-start.1 = ((bf16[32,128,16]{1,2,0:T(8,128)(2,1)}), bf16[32,128,16]{1,2,0:T(8,128)(2,1)}, u32[]{:S(2)}, u32[]{:S(2)}) async-start(bf16[32,128,16]{1,2,0:T(8,128)(2,1)} %broadcast_in_dim.56), calls=%async_computation.1 | async-start | bytes 262144 | tf_op jit(solution)/shard_map/all_to_all | solution.py:500
  57.2 5.2 %collective-permute-done.refs_0_ = bf16[128,3584]{1,0:T(8,128)(2,1)} collective-permute-done((bf16[128,3584]{1,0:T(8,128)(2,1)}, bf16[128,3584]{1,0:T(8,128)(2,1)}, u32[]{:S(2)}, u32[]{:S(2)}) %collective-permute-start) | collective-permute-done | bytes 917536 | tf_op jit(solution)/shard_map/ppermute | solution.py:488
  62.4 11.9 %collective-permute-done.5.refs_5_.refs_0_ = bf16[128,3584]{1,0:T(8,128)(2,1)} collective-permute-done((bf16[128,3584]{1,0:T(8,128)(2,1)}, bf16[128,3584]{1,0:T(8,128)(2,1)}, u32[]{:S(2)}, u32[]{:S(2)}) %collective-permute-start.5) | collective-permute-done | bytes 917536 | tf_op jit(solution)/shard_map/ppermute | solution.py:488
  81.0 3.1 %shard_map.157 = bf16[2,3,48,512]{3,2,1,0:T(8,128)(2,1)} custom-call(bf16[32,16]{1,0:T(8,128)(2,1)} %pad_convert_fusion.columns_ref, bf16[128,16]{1,0:T(8,128)(2,1)} %copy.68.refs_6_.gates_ref, bf16[16,48,1024]{2,1,0:T(8,128)(2,1)} %get-tuple-element.42.rows_ref, f32[144,768]{1,0:T(8,128)} %copy.70.pairs_ref), custom_call_target="tpu_custom_call" | custom-call | flops 1 | bytes 1 | tf_op jit(solution)/shard_map/pallas_call | solution.py:191
  89.2 4.8 %shard_map.158 = (bf16[2,8,2,48,128]{4,3,2,1,0:T(8,128)(2,1)}, bf16[2,8,2,48,128]{4,3,2,1,0:T(8,128)(2,1)}, bf16[2,8,2,48,128]{4,3,2,1,0:T(8,128)(2,1)}) custom-call(bf16[16,16]{1,0:T(8,128)(2,1)} %fusion.6.columns_ref, bf16[8,128,16]{2,1,0:T(8,128)(2,1)} %bitcast.49, bf16[8,128,16]{2,1,0:T(8,128)(2,1)} %bitcast.48), custom_call_target="tpu_custom_call" | custom-call | flops 1 | bytes 1 | tf_op jit(solution)/shard_map/pallas_call | solution.py:103
  94.0 4.5 %collective-permute-done.10.refs_5_ = bf16[3,48,512]{2,1,0:T(8,128)(2,1)S(1)} collective-permute-done((bf16[3,48,512]{2,1,0:T(8,128)(2,1)S(1)}, bf16[3,48,512]{2,1,0:T(8,128)(2,1)S(1)}, u32[]{:S(2)}, u32[]{:S(2)}) %collective-permute-start.10) | collective-permute-done | bytes 147488 | tf_op jit(solution)/shard_map/ppermute | solution.py:482
  98.5 3.8 %collective-permute-done.6.refs_1_ = bf16[128,3584]{1,0:T(8,128)(2,1)S(1)} collective-permute-done((bf16[128,3584]{1,0:T(8,128)(2,1)}, bf16[128,3584]{1,0:T(8,128)(2,1)S(1)}, u32[]{:S(2)}, u32[]{:S(2)}) %collective-permute-start.6) | collective-permute-done | bytes 917536 | tf_op jit(solution)/shard_map/ppermute | solution.py:549
  103.9 4.7 %shard_map.160.refs_7_.refs_5_.refs_6_ = bf16[2,256,3584]{2,1,0:T(8,128)(2,1)} custom-call(f32[2,256,3584]{2,1,0:T(8,128)} %refs_9_.1, bf16[128,3584]{1,0:T(8,128)(2,1)} %get-tuple-element.45.refs_1_), custom_call_target="tpu_custom_call" | custom-call | flops 1 | bytes 1 | tf_op jit(solution)/shard_map/pallas_call | solution.py:138
  109.4 1.7 collective-permute-start.14
  113.3 18.2 %collective-permute-done.15.refs_3_ = bf16[128,3584]{1,0:T(8,128)(2,1)S(1)} collective-permute-done((bf16[128,3584]{1,0:T(8,128)(2,1)S(1)}, bf16[128,3584]{1,0:T(8,128)(2,1)S(1)}, u32[]{:S(2)}, u32[]{:S(2)}) %collective-permute-start.15) | collective-permute-done | bytes 917536 | tf_op jit(solution)/shard_map/ppermute | solution.py:482
  131.9 3.2 %collective-permute-done.13.refs_1_ = bf16[128,3584]{1,0:T(8,128)(2,1)S(1)} collective-permute-done((bf16[128,3584]{1,0:T(8,128)(2,1)S(1)}, bf16[128,3584]{1,0:T(8,128)(2,1)S(1)}, u32[]{:S(2)}, u32[]{:S(2)}) %collective-permute-start.13) | collective-permute-done | bytes 917536 | tf_op jit(solution)/shard_map/ppermute | solution.py:549
  136.4 7.9 %collective-permute-done.25 = bf16[2,3,48,512]{3,2,1,0:T(8,128)(2,1)S(1)} collective-permute-done((bf16[2,3,48,512]{3,2,1,0:T(8,128)(2,1)}, bf16[2,3,48,512]{3,2,1,0:T(8,128)(2,1)S(1)}, u32[]{:S(2)}, u32[]{:S(2)}) %collective-permute-start.25) | collective-permute-done | bytes 294944 | tf_op jit(solution)/shard_map/ppermute | solution.py:488
  148.4 16.7 %shard_map.161 = (bf16[5,2,48,512]{3,2,1,0:T(8,128)(2,1)}, bf16[2,2,48,512]{3,2,1,0:T(8,128)(2,1)}, f32[2,7,128]{2,1,0:T(8,128)}, bf16[896,3584]{1,0:T(8,128)(2,1)}) custom-call(s32[8]{0:T(128)} %fusion.8.peers_ref, s32[1]{0:T(128)} %bitcast.1.core_ref.chunk_ref, bf16[128,3584]{1,0:T(8,128)(2,1)} %refs_0_.3, bf16[128,3584]{1,0:T(8,128)(2,1)} %get-tuple-element.40.refs_1_, ...), custom_call_target="tpu_custom_call" | custom-call | flops 6576668672 | bytes 20185088 | tf_op jit(solution)/shard_map/pallas_call | solution.py:257
  165.1 1.9 collective-permute-done.12.refs_4_.refs_1_
  167.8 2.2 broadcast_select_fusion.refs_4_
  173.6 1.9 slice.19
  178.4 12.9 %shard_map.163 = (bf16[2,2,48,512]{3,2,1,0:T(8,128)(2,1)}, bf16[3,2,48,512]{3,2,1,0:T(8,128)(2,1)}, f32[2,5,128]{2,1,0:T(8,128)}, bf16[640,3584]{1,0:T(8,128)(2,1)}) custom-call(s32[8]{0:T(128)} %fusion.8.peers_ref, s32[1]{0:T(128)} %bitcast.1.core_ref.chunk_ref, bf16[128,3584]{1,0:T(8,128)(2,1)} %collective-permute-done.5.refs_5_.refs_0_, ...), custom_call_target="tpu_custom_call" | custom-call | flops 4697620480 | bytes 16515072 | tf_op jit(solution)/shard_map/pallas_call | solution.py:257
  191.4 8.3 %collective-permute-done.19.refs_3_ = bf16[64,3584]{1,0:T(8,128)(2,1)S(1)} collective-permute-done((bf16[64,3584]{1,0:T(8,128)(2,1)}, bf16[64,3584]{1,0:T(8,128)(2,1)S(1)}, u32[]{:S(2)}, u32[]{:S(2)}) %collective-permute-start.19) | collective-permute-done | bytes 458784 | tf_op jit(solution)/shard_map/ppermute | solution.py:482
  206.0 6.6 %shard_map.168.refs_2_ = bf16[1024,2048]{1,0:T(8,128)(2,1)} custom-call(s32[16,2]{1,0:T(8,128)} %shard_map.166.places_ref, s32[2]{0:T(128)} %copy-done.41, bf16[2,8,2,48,128]{4,3,2,1,0:T(8,128)(2,1)} %get-tuple-element.43.refs_6_.scale_ref, bf16[8,2,48,512]{3,2,1,0:T(8,128)(2,1)} %get-tuple-element.50.refs_11_.refs_9_.refs_10_.nr_ref, ...), custom_call_target="tpu_custom_call" | custom-call | flops 1 | bytes 1 | tf_op jit(solution)/shard_map/pallas_call | solution.py:346
  212.6 18.2 %shard_map.169 = bf16[1024,3584]{1,0:T(8,128)(2,1)} custom-call(bf16[896,3584]{1,0:T(8,128)(2,1)} %get-tuple-element.67.refs_0_, bf16[640,3584]{1,0:T(8,128)(2,1)} %get-tuple-element.68.refs_1_, bf16[1024,2048]{1,0:T(8,128)(2,1)} %shard_map.168.refs_2_), custom_call_target="tpu_custom_call" | custom-call | flops 15032385536 | bytes 22020096 | tf_op jit(solution)/shard_map/pallas_call | solution.py:379
  231.8 7.2 %shard_map.170 = bf16[2,256,3584]{2,1,0:T(8,128)(2,1)} custom-call(s32[1]{0:T(128)S(6)} %sub.12.chunk_ref, bf16[128,3584]{1,0:T(8,128)(2,1)} %get-tuple-element.60.refs_0_, bf16[128,3584]{1,0:T(8,128)(2,1)} %get-tuple-element.61.refs_1_, bf16[64,3584]{1,0:T(8,128)(2,1)} %copy-done.13, bf16[64,3584]{1,0:T(8,128)(2,1)} %copy-done.12, ...), custom_call_target="tpu_custom_call" | custom-call | flops 1 | bytes 1 | tf_op jit(solution)/shard_map/pallas_call | solution.py:424
  241.9 10.1 %shard_map.165 = (bf16[1,2,48,512]{3,2,1,0:T(8,128)(2,1)}, bf16[3,2,48,512]{3,2,1,0:T(8,128)(2,1)}, f32[2,4,128]{2,1,0:T(4,128)}) custom-call(s32[8]{0:T(128)} %fusion.8.peers_ref, s32[1]{0:T(128)} %bitcast.1.core_ref.chunk_ref, bf16[128,3584]{1,0:T(8,128)(2,1)} %get-tuple-element.60.refs_0_, bf16[128,3584]{1,0:T(8,128)(2,1)} %get-tuple-element.61.refs_1_, ...), custom_call_target="tpu_custom_call" | custom-call | flops 3758096384 | bytes 14680064 | tf_op jit(solution)/shard_map/pallas_call | solution.py:257
  255.6 3.7 %all-to-all-start.2 = ((f32[16,2,128]{2,1,0:T(2,128)}), f32[16,2,128]{2,1,0:T(2,128)S(1)}, u32[]{:S(2)}, u32[]{:S(2)}) async-start(f32[16,2,128]{2,1,0:T(2,128)} %bitcast.22), calls=%async_computation.2 | async-start | bytes 32768 | tf_op jit(solution)/shard_map/all_to_all | solution.py:662
  259.3 19.6 %shard_map.171 = (f32[2,256,3584]{2,1,0:T(8,128)}, bf16[2,256,3584]{2,1,0:T(8,128)(2,1)}, bf16[2,256,3584]{2,1,0:T(8,128)(2,1)}) custom-call(s32[1]{0:T(128)} %bitcast.1.core_ref.chunk_ref, bf16[128,3584]{1,0:T(8,128)(2,1)} %get-tuple-element.60.refs_0_, bf16[128,3584]{1,0:T(8,128)(2,1)} %get-tuple-element.61.refs_1_, bf16[64,3584]{1,0:T(8,128)(2,1)} %copy-done.13, ...), custom_call_target="tpu_custom_call" | custom-call | flops 1879048192 | bytes 47710208 | tf_op jit(solution)/shard_map/pallas_call | solution.py:424
  283.2 3.4 %shard_map.172 = bf16[8,2,48,1024]{3,2,1,0:T(8,128)(2,1)} custom-call(s32[8]{0:T(128)} %fusion.8.peers_ref, s32[1]{0:T(128)} %bitcast.plane_ref, bf16[5,2,48,512]{3,2,1,0:T(8,128)(2,1)} %get-tuple-element.51.refs_0_, bf16[2,2,48,512]{3,2,1,0:T(8,128)(2,1)} %get-tuple-element.58.refs_1_, bf16[1,2,48,512]{3,2,1,0:T(8,128)(2,1)} %get-tuple-element.62.refs_2_, ...), custom_call_target="tpu_custom_call" | custom-call | flops 1 | bytes 1 | tf_op jit(solution)/shard_map/pallas_call | solution.py:311
  (198 shorter events, 51.9 us)
Async XLA Ops:
  7.2 45.9 %all-to-all-start = ((bf16[8,2,48,1024]{3,2,1,0:T(8,128)(2,1)}), bf16[8,2,48,1024]{3,2,1,0:T(8,128)(2,1)S(1)}, u32[]{:S(2)}, u32[]{:S(2)}) async-start(bf16[8,2,48,1024]{3,2,1,0:T(8,128)(2,1)} %bitcast.43), calls=%async_computation | async-start | bytes 3145728 | tf_op jit(solution)/shard_map/all_to_all | solution.py:561
  14.6 23.6 %collective-permute-start.4 = (bf16[128,3584]{1,0:T(8,128)(2,1)}, bf16[128,3584]{1,0:T(8,128)(2,1)}, u32[]{:S(2)}, u32[]{:S(2)}) collective-permute-start(bf16[128,3584]{1,0:T(8,128)(2,1)} %refs_0_.3), channel_id=1, source_target_pairs={{0,16},{8,24},{16,0},{24,8},{1,17},{9,25},{17,1},{25,9},{2,18},{10... | collective-permute-start | bytes 2752520 | tf_op jit(solution)/shard_map/ppermute | solution.py:482
  16.1 41.0 %collective-permute-start.2 = (bf16[128,3584]{1,0:T(8,128)(2,1)}, bf16[128,3584]{1,0:T(8,128)(2,1)}, u32[]{:S(2)}, u32[]{:S(2)}) collective-permute-start(bf16[128,3584]{1,0:T(8,128)(2,1)} %refs_0_.3), channel_id=1, source_target_pairs={{0,1},{1,0},{2,3},{3,2},{4,5},{5,4},{6,7},{7,6},{8,9},{9,8},{10,11... | collective-permute-start | bytes 2752520 | tf_op jit(solution)/shard_map/ppermute | solution.py:488
  18.1 39.0 %collective-permute-start.1 = (bf16[128,3584]{1,0:T(8,128)(2,1)}, bf16[128,3584]{1,0:T(8,128)(2,1)S(1)}, u32[]{:S(2)}, u32[]{:S(2)}) collective-permute-start(bf16[128,3584]{1,0:T(8,128)(2,1)} %refs_0_.3), channel_id=1, source_target_pairs={{2,4},{3,5},{4,2},{5,3},{10,12},{11,13},{12,10},{13,11},{18,20},{1... | collective-permute-start | bytes 2752520 | tf_op jit(solution)/shard_map/ppermute | solution.py:549
  18.9 43.6 %collective-permute-start = (bf16[128,3584]{1,0:T(8,128)(2,1)}, bf16[128,3584]{1,0:T(8,128)(2,1)}, u32[]{:S(2)}, u32[]{:S(2)}) collective-permute-start(bf16[128,3584]{1,0:T(8,128)(2,1)} %refs_0_.3), channel_id=1, source_target_pairs={{0,2},{1,3},{2,0},{3,1},{4,6},{5,7},{6,4},{7,5},{8,10},{9,11},{10,... | collective-permute-start | bytes 2752520 | tf_op jit(solution)/shard_map/ppermute | solution.py:488
  25.4 31.8 %collective-permute-start.3 = (bf16[8,2,48,512]{3,2,1,0:T(8,128)(2,1)}, bf16[8,2,48,512]{3,2,1,0:T(8,128)(2,1)S(1)}, u32[]{:S(2)}, u32[]{:S(2)}) collective-permute-start(bf16[8,2,48,512]{3,2,1,0:T(8,128)(2,1)} %get-tuple-element.39), channel_id=1, source_target_pairs={{0,16},{8,24},{16,0},{24,8},{1,17},{9,25},{17,1},{25,9},{2,18},{10... | collective-permute-start | bytes 2359304 | tf_op jit(solution)/shard_map/ppermute | solution.py:482
  26.1 53.7 %copy-start.38 = (s32[16]{0:T(128)}, s32[16]{0:T(128)S(1)}, u32[]{:S(2)}) copy-start(s32[16]{0:T(128)S(1)} %convert_reduce_fusion) | copy-start | bytes 196
  38.2 36.1 %collective-permute-start.5 = (bf16[128,3584]{1,0:T(8,128)(2,1)}, bf16[128,3584]{1,0:T(8,128)(2,1)}, u32[]{:S(2)}, u32[]{:S(2)}) collective-permute-start(bf16[128,3584]{1,0:T(8,128)(2,1)} %collective-permute-done.4.refs_2_), channel_id=1, source_target_pairs={{0,1},{1,0},{2,3},{3,2},{4,5},{5,4},{6,7},{7,6},{8,9},{9,8},{10,11... | collective-permute-start | bytes 2752520 | tf_op jit(solution)/shard_map/ppermute | solution.py:488
  53.8 32.9 %all-to-all-start.1 = ((bf16[32,128,16]{1,2,0:T(8,128)(2,1)}), bf16[32,128,16]{1,2,0:T(8,128)(2,1)}, u32[]{:S(2)}, u32[]{:S(2)}) async-start(bf16[32,128,16]{1,2,0:T(8,128)(2,1)} %broadcast_in_dim.56), calls=%async_computation.1 | async-start | bytes 262144 | tf_op jit(solution)/shard_map/all_to_all | solution.py:500
  57.1 148.9 %all-gather.3.cloned.1.call-start = ((), (), s32[]{:S(2)}) async-start(), calls=%async_computation.3 | async-start | bytes 2949120 | tf_op jit(solution)/shard_map/all_gather | solution.py:609
  74.4 27.9 %collective-permute-start.9 = (bf16[128,3584]{1,0:T(8,128)(2,1)}, bf16[128,3584]{1,0:T(8,128)(2,1)S(1)}, u32[]{:S(2)}, u32[]{:S(2)}) collective-permute-start(bf16[128,3584]{1,0:T(8,128)(2,1)} %get-tuple-element.40.refs_1_), channel_id=1, source_target_pairs={{0,16},{8,24},{16,0},{24,8},{1,17},{9,25},{17,1},{25,9},{2,18},{10... | collective-permute-start | bytes 2752520 | tf_op jit(solution)/shard_map/ppermute | solution.py:482
  76.0 26.3 %collective-permute-start.8 = (bf16[128,3584]{1,0:T(8,128)(2,1)}, bf16[128,3584]{1,0:T(8,128)(2,1)}, u32[]{:S(2)}, u32[]{:S(2)}) collective-permute-start(bf16[128,3584]{1,0:T(8,128)(2,1)} %get-tuple-element.40.refs_1_), channel_id=1, source_target_pairs={{0,1},{1,0},{2,3},{3,2},{4,5},{5,4},{6,7},{7,6},{8,9},{9,8},{10,11... | collective-permute-start | bytes 2752520 | tf_op jit(solution)/shard_map/ppermute | solution.py:488
  76.3 26.1 %collective-permute-start.7 = (bf16[128,3584]{1,0:T(8,128)(2,1)}, bf16[128,3584]{1,0:T(8,128)(2,1)S(1)}, u32[]{:S(2)}, u32[]{:S(2)}) collective-permute-start(bf16[128,3584]{1,0:T(8,128)(2,1)} %get-tuple-element.40.refs_1_), channel_id=1, source_target_pairs={{2,4},{3,5},{4,2},{5,3},{10,12},{11,13},{12,10},{13,11},{18,20},{1... | collective-permute-start | bytes 2752520 | tf_op jit(solution)/shard_map/ppermute | solution.py:549
  77.0 25.3 %collective-permute-start.6 = (bf16[128,3584]{1,0:T(8,128)(2,1)}, bf16[128,3584]{1,0:T(8,128)(2,1)S(1)}, u32[]{:S(2)}, u32[]{:S(2)}) collective-permute-start(bf16[128,3584]{1,0:T(8,128)(2,1)} %get-tuple-element.41.refs_0_), channel_id=1, source_target_pairs={{2,0},{3,1},{4,6},{5,7},{10,8},{11,9},{12,14},{13,15},{18,16},{19,... | collective-permute-start | bytes 2752520 | tf_op jit(solution)/shard_map/ppermute | solution.py:549
  85.7 12.8 %collective-permute-start.10 = (bf16[3,48,512]{2,1,0:T(8,128)(2,1)S(1)}, bf16[3,48,512]{2,1,0:T(8,128)(2,1)S(1)}, u32[]{:S(2)}, u32[]{:S(2)}) collective-permute-start(bf16[3,48,512]{2,1,0:T(8,128)(2,1)S(1)} %get-tuple-element.76), channel_id=1, source_target_pairs={{0,16},{8,24},{16,0},{24,8},{1,17},{9,25},{17,1},{25,9},{2,18},{10... | collective-permute-start | bytes 442376 | tf_op jit(solution)/shard_map/ppermute | solution.py:482
  108.6 39.7 %collective-permute-start.11 = (bf16[2,256,3584]{2,1,0:T(8,128)(2,1)}, bf16[2,256,3584]{2,1,0:T(8,128)(2,1)}, u32[]{:S(2)}, u32[]{:S(2)}) collective-permute-start(bf16[2,256,3584]{2,1,0:T(8,128)(2,1)} %shard_map.160.refs_7_.refs_5_.refs_6_), channel_id=1, source_target_pairs={{0,8},{8,0},{16,24},{24,16},{1,9},{9,1},{17,25},{25,17},{2,10},{10... | collective-permute-start | bytes 11010056 | tf_op jit(solution)/shard_map/ppermute | solution.py:485
  108.8 22.8 %collective-permute-start.15 = (bf16[128,3584]{1,0:T(8,128)(2,1)S(1)}, bf16[128,3584]{1,0:T(8,128)(2,1)S(1)}, u32[]{:S(2)}, u32[]{:S(2)}) collective-permute-start(bf16[128,3584]{1,0:T(8,128)(2,1)S(1)} %broadcast_select_fusion.1.refs_4_), channel_id=1, source_target_pairs={{0,16},{8,24},{16,0},{24,8},{1,17},{9,25},{17,1},{25,9},{2,18},{10... | collective-permute-start | bytes 2752520 | tf_op jit(solution)/shard_map/ppermute | solution.py:482
  109.4 22.6 %collective-permute-start.14 = (bf16[128,3584]{1,0:T(8,128)(2,1)S(1)}, bf16[128,3584]{1,0:T(8,128)(2,1)}, u32[]{:S(2)}, u32[]{:S(2)}) collective-permute-start(bf16[128,3584]{1,0:T(8,128)(2,1)S(1)} %broadcast_select_fusion.1.refs_4_), channel_id=1, source_target_pairs={{0,1},{1,0},{2,3},{3,2},{4,5},{5,4},{6,7},{7,6},{8,9},{9,8},{10,11... | collective-permute-start | bytes 2752520 | tf_op jit(solution)/shard_map/ppermute | solution.py:488
  111.1 24.1 %collective-permute-start.13 = (bf16[128,3584]{1,0:T(8,128)(2,1)S(1)}, bf16[128,3584]{1,0:T(8,128)(2,1)S(1)}, u32[]{:S(2)}, u32[]{:S(2)}) collective-permute-start(bf16[128,3584]{1,0:T(8,128)(2,1)S(1)} %copy-done.7), channel_id=1, source_target_pairs={{2,0},{3,1},{4,6},{5,7},{10,8},{11,9},{12,14},{13,15},{18,16},{19,... | collective-permute-start | bytes 2752520 | tf_op jit(solution)/shard_map/ppermute | solution.py:549
  136.1 8.2 %collective-permute-start.25 = (bf16[2,3,48,512]{3,2,1,0:T(8,128)(2,1)}, bf16[2,3,48,512]{3,2,1,0:T(8,128)(2,1)S(1)}, u32[]{:S(2)}, u32[]{:S(2)}) collective-permute-start(bf16[2,3,48,512]{3,2,1,0:T(8,128)(2,1)} %shard_map.167), channel_id=1, source_target_pairs={{0,1},{1,0},{2,3},{3,2},{4,5},{5,4},{6,7},{7,6},{8,9},{9,8},{10,11... | collective-permute-start | bytes 884744 | tf_op jit(solution)/shard_map/ppermute | solution.py:488
  146.2 20.7 %collective-permute-start.12 = (bf16[128,3584]{1,0:T(8,128)(2,1)}, bf16[128,3584]{1,0:T(8,128)(2,1)S(1)}, u32[]{:S(2)}, u32[]{:S(2)}) collective-permute-start(bf16[128,3584]{1,0:T(8,128)(2,1)} %get-tuple-element.46.refs_5_), channel_id=1, source_target_pairs={{0,16},{8,24},{16,0},{24,8},{1,17},{9,25},{17,1},{25,9},{2,18},{10... | collective-permute-start | bytes 2752520 | tf_op jit(solution)/shard_map/ppermute | solution.py:482
  170.1 30.8 %collective-permute-start.17 = (bf16[128,3584]{1,0:T(8,128)(2,1)}, bf16[128,3584]{1,0:T(8,128)(2,1)S(1)}, u32[]{:S(2)}, u32[]{:S(2)}) collective-permute-start(bf16[128,3584]{1,0:T(8,128)(2,1)} %broadcast_select_fusion.refs_4_), channel_id=1, source_target_pairs={{0,16},{8,24},{16,0},{24,8},{1,17},{9,25},{17,1},{25,9},{2,18},{10... | collective-permute-start | bytes 2752520 | tf_op jit(solution)/shard_map/ppermute | solution.py:482
  171.6 29.4 %collective-permute-start.16 = (bf16[128,3584]{1,0:T(8,128)(2,1)}, bf16[128,3584]{1,0:T(8,128)(2,1)S(1)}, u32[]{:S(2)}, u32[]{:S(2)}) collective-permute-start(bf16[128,3584]{1,0:T(8,128)(2,1)} %broadcast_select_fusion.refs_4_), channel_id=1, source_target_pairs={{0,1},{1,0},{2,3},{3,2},{4,5},{5,4},{6,7},{7,6},{8,9},{9,8},{10,11... | collective-permute-start | bytes 2752520 | tf_op jit(solution)/shard_map/ppermute | solution.py:488
  175.5 24.3 %collective-permute-start.19 = (bf16[64,3584]{1,0:T(8,128)(2,1)}, bf16[64,3584]{1,0:T(8,128)(2,1)S(1)}, u32[]{:S(2)}, u32[]{:S(2)}) collective-permute-start(bf16[64,3584]{1,0:T(8,128)(2,1)} %slice.19), channel_id=1, source_target_pairs={{0,16},{8,24},{16,0},{24,8},{1,17},{9,25},{17,1},{25,9},{2,18},{10... | collective-permute-start | bytes 1376264 | tf_op jit(solution)/shard_map/ppermute | solution.py:482
  176.0 24.9 %collective-permute-start.18 = (bf16[64,3584]{1,0:T(8,128)(2,1)S(1)}, bf16[64,3584]{1,0:T(8,128)(2,1)S(1)}, u32[]{:S(2)}, u32[]{:S(2)}) collective-permute-start(bf16[64,3584]{1,0:T(8,128)(2,1)S(1)} %slice.18), channel_id=1, source_target_pairs={{0,1},{1,0},{2,3},{3,2},{4,5},{5,4},{6,7},{7,6},{8,9},{9,8},{10,11... | collective-permute-start | bytes 1376264 | tf_op jit(solution)/shard_map/ppermute | solution.py:488
  205.1 25.8 %collective-permute-start.21 = (bf16[64,3584]{1,0:T(8,128)(2,1)S(1)}, bf16[64,3584]{1,0:T(8,128)(2,1)S(1)}, u32[]{:S(2)}, u32[]{:S(2)}) collective-permute-start(bf16[64,3584]{1,0:T(8,128)(2,1)S(1)} %slice.21), channel_id=1, source_target_pairs={{0,16},{8,24},{16,0},{24,8},{1,17},{9,25},{17,1},{25,9},{2,18},{10... | collective-permute-start | bytes 1376264 | tf_op jit(solution)/shard_map/ppermute | solution.py:482
  205.7 25.2 %collective-permute-start.20 = (bf16[64,3584]{1,0:T(8,128)(2,1)S(1)}, bf16[64,3584]{1,0:T(8,128)(2,1)S(1)}, u32[]{:S(2)}, u32[]{:S(2)}) collective-permute-start(bf16[64,3584]{1,0:T(8,128)(2,1)S(1)} %slice.20), channel_id=1, source_target_pairs={{0,1},{1,0},{2,3},{3,2},{4,5},{5,4},{6,7},{7,6},{8,9},{9,8},{10,11... | collective-permute-start | bytes 1376264 | tf_op jit(solution)/shard_map/ppermute | solution.py:488
  239.0 20.3 %collective-permute-start.26 = (bf16[2,256,3584]{2,1,0:T(8,128)(2,1)}, bf16[2,256,3584]{2,1,0:T(8,128)(2,1)}, u32[]{:S(2)}, u32[]{:S(2)}) collective-permute-start(bf16[2,256,3584]{2,1,0:T(8,128)(2,1)} %shard_map.170), channel_id=1, source_target_pairs={{0,8},{8,0},{16,24},{24,16},{1,9},{9,1},{17,25},{25,17},{2,10},{10... | collective-permute-start | bytes 11010056 | tf_op jit(solution)/shard_map/ppermute | solution.py:485
  239.8 42.4 %collective-permute-start.22 = (bf16[2,2,48,512]{3,2,1,0:T(8,128)(2,1)S(1)}, bf16[2,2,48,512]{3,2,1,0:T(8,128)(2,1)S(1)}, u32[]{:S(2)}, u32[]{:S(2)}) collective-permute-start(bf16[2,2,48,512]{3,2,1,0:T(8,128)(2,1)S(1)} %copy-done.45), channel_id=1, source_target_pairs={{0,16},{8,24},{16,0},{24,8},{1,17},{9,25},{17,1},{25,9},{2,18},{10... | collective-permute-start | bytes 589832 | tf_op jit(solution)/shard_map/ppermute | solution.py:482
  241.4 40.9 %collective-permute-start.23 = (bf16[3,2,48,512]{3,2,1,0:T(8,128)(2,1)S(1)}, bf16[3,2,48,512]{3,2,1,0:T(8,128)(2,1)S(1)}, u32[]{:S(2)}, u32[]{:S(2)}) collective-permute-start(bf16[3,2,48,512]{3,2,1,0:T(8,128)(2,1)S(1)} %copy-done.44), channel_id=1, source_target_pairs={{0,16},{8,24},{16,0},{24,8},{1,17},{9,25},{17,1},{25,9},{2,18},{10... | collective-permute-start | bytes 884744 | tf_op jit(solution)/shard_map/ppermute | solution.py:482
  252.8 29.5 %collective-permute-start.24 = (bf16[3,2,48,512]{3,2,1,0:T(8,128)(2,1)}, bf16[3,2,48,512]{3,2,1,0:T(8,128)(2,1)S(1)}, u32[]{:S(2)}, u32[]{:S(2)}) collective-permute-start(bf16[3,2,48,512]{3,2,1,0:T(8,128)(2,1)} %get-tuple-element.65), channel_id=1, source_target_pairs={{0,16},{8,24},{16,0},{24,8},{1,17},{9,25},{17,1},{25,9},{2,18},{10... | collective-permute-start | bytes 884744 | tf_op jit(solution)/shard_map/ppermute | solution.py:482
  255.6 23.4 %all-to-all-start.2 = ((f32[16,2,128]{2,1,0:T(2,128)}), f32[16,2,128]{2,1,0:T(2,128)S(1)}, u32[]{:S(2)}, u32[]{:S(2)}) async-start(f32[16,2,128]{2,1,0:T(2,128)} %bitcast.22), calls=%async_computation.2 | async-start | bytes 32768 | tf_op jit(solution)/shard_map/all_to_all | solution.py:662
  (45 other events, 342.1 us)
Sparse Core Ops, SparseCore 0:
  146.3 48.7 all-gather.2
